TPU v7x, 128 devices: a whole 4x4x4 slice. The times are simulated.
128 devices in a mesh: lon: 32 (over y, z, x_lo), lat: 4 (over x_hi, core).
Axes of the slice: x: 4 (x_hi: 2, x_lo: 2; x = x_hi * 2 + x_lo), y: 4, z: 4, core: 2. Of those that a mesh axis runs over, the one named last changes fastest.
Arguments:
- latent_state: bfloat16 [512, 64, 512], P('lon', 'lat'), may hold values from -6 to 6
- cotangent: bfloat16 [512, 64, 512], P('lon', 'lat'), may hold values from -6 to 6
- w_inner: bfloat16 [512, 1024], replicated, may hold values from -0.25 to 0.25
- w_outer: bfloat16 [1024, 512], replicated, may hold values from -0.1875 to 0.1875
- norm_gain: float32 [512], replicated, may hold values from 0.5 to 1.5
- source_block: int32 [512, 64], P('lon', 'lat'), may hold values from 0 to 127, as said below
- corner_code: int32 [512, 64], P('lon', 'lat'), may hold values from 0 to 54, as said below
- frac_lon: float32 [512, 64], P('lon', 'lat'), may hold values from 0 to 1
- frac_lat: float32 [512, 64], P('lon', 'lat'), may hold values from 0 to 1
- terrain: int32 [512, 64], P('lon', 'lat'), may hold values from 0 to 7
- kappa_table: float32 [8], replicated, may hold values from 0.05 to 0.24
Outputs:
- state_out: bfloat16 [512, 64, 512], P('lon', 'lat')
- state_grad: bfloat16 [512, 64, 512], P('lon', 'lat')
- grad_inner: float32 [512, 1024], replicated
- grad_outer: float32 [1024, 512], replicated
- grad_gain: float32 [512], replicated
Inputs may be any that keep to these rules, and one draw needn't show every extreme that they name: `source_block`: the block's latitude part lies in the target's own lat tile; values run over all 8 x 8 blocks of that tile row. Row corner_code // 8 and column corner_code % 8 are both at most 6.
All inputs are finite; a program needn't handle non-finite values.
Results may differ from a plain program's by a relative error of at most 0.017.
Values may be sent and summed in bfloat16 or wider, within the bound.
A program may use at most 128 MiB of HBM per device.

v0:
```python
import jax
import jax.numpy as jnp
from jax import lax
from jax.sharding import PartitionSpec as P

STEPS = 4


def with_halo(value, sides, width, wrap):
    for axis, dim in sides:
        size, length = (lax.axis_size(axis), value.shape[dim])
        up = [(i, (i + 1) % size) for i in range(size if wrap else size - 1)]
        down = [(j, i) for i, j in up]
        last = lax.slice_in_dim(value, length - width, length, axis=dim)
        first = lax.slice_in_dim(value, 0, width, axis=dim)
        before = lax.ppermute(last, axis, up)
        after = lax.ppermute(first, axis, down)
        value = jnp.concatenate([before, value, after], axis=dim)
    return value


def flat_sources(source_block, corner_code, lat_cells):
    per_row = lat_cells // 8
    lon_part = source_block // per_row * 8 + corner_code // 8
    lat_part = source_block % per_row * 8 + corner_code % 8
    return lon_part * lat_cells + lat_part


def corner_table(flat_ids, frac_a, frac_b, lat_cells):
    shifted = jnp.stack([flat_ids, flat_ids + lat_cells, flat_ids + 1, flat_ids + lat_cells + 1])
    weights = jnp.stack(
        [
            (1.0 - frac_a) * (1.0 - frac_b),
            frac_a * (1.0 - frac_b),
            (1.0 - frac_a) * frac_b,
            frac_a * frac_b,
        ]
    )
    return (shifted, weights)


def laplace(field):
    wide = with_halo(field.astype(jnp.bfloat16), (("lon", 0),), 1, True).astype(field.dtype)
    tall = with_halo(field.astype(jnp.bfloat16), (("lat", 1),), 1, False).astype(field.dtype)
    return wide[2:] + wide[:-2] + tall[:, 2:] + tall[:, :-2] - 4.0 * field


def on_device(
    latent_state,
    cotangent,
    w_inner,
    w_outer,
    norm_gain,
    source_block,
    corner_code,
    frac_lon,
    frac_lat,
    terrain,
    kappa_table,
):
    lon_cells, lat_cells, chans = latent_state.shape
    cells = lon_cells * lat_cells
    flat_ids = flat_sources(source_block, corner_code, lat_cells)
    shifted, weights = corner_table(
        flat_ids.reshape(cells), frac_lon.reshape(cells), frac_lat.reshape(cells), lat_cells
    )
    shard_piece = lax.all_gather(latent_state, "lon", axis=0, tiled=True)
    count = shard_piece.shape[0] * lat_cells
    local = shifted
    hits = local[:, :, None] == jnp.arange(count, dtype=jnp.int32)[None, None, :]
    select = jnp.sum(jnp.where(hits, weights[:, :, None], 0.0), 0)
    upper = select.astype(jnp.bfloat16)
    lower = (select - upper.astype(jnp.float32)).astype(jnp.bfloat16)
    values = shard_piece.reshape(count, chans)
    running = jnp.dot(upper, values, preferred_element_type=jnp.float32)
    drift = running + jnp.dot(lower, values, preferred_element_type=jnp.float32)
    drift = drift.reshape(lon_cells, lat_cells, chans)
    classes = jnp.arange(kappa_table.shape[0], dtype=jnp.int32)
    kappa = jnp.sum(jnp.where(terrain[..., None] == classes, kappa_table, 0.0), -1)[..., None]
    field = drift
    for turn_index in range(STEPS):
        field = field + kappa * laplace(field)
    flat_field = field.reshape(cells, chans)
    rstd = lax.rsqrt(jnp.mean(flat_field * flat_field, -1, keepdims=True) + 1e-06)
    normed = flat_field * rstd
    z_in = (normed * norm_gain).astype(jnp.bfloat16)
    pre_act = jnp.dot(z_in, w_inner, preferred_element_type=jnp.float32)
    act = jax.nn.silu(pre_act).astype(jnp.bfloat16)
    react = jnp.dot(act, w_outer, preferred_element_type=jnp.float32)
    state_out = (flat_field + react).astype(jnp.bfloat16).reshape(lon_cells, lat_cells, chans)
    cot = cotangent.reshape(cells, chans)
    local_outer = jnp.dot(act.T, cot, preferred_element_type=jnp.float32)
    grad_act = jnp.dot(cot, w_outer.T, preferred_element_type=jnp.float32)
    sigma = jax.nn.sigmoid(pre_act)
    grad_pre = (grad_act * sigma * (1.0 + pre_act * (1.0 - sigma))).astype(jnp.bfloat16)
    local_inner = jnp.dot(z_in.T, grad_pre, preferred_element_type=jnp.float32)
    grad_z = jnp.dot(grad_pre, w_inner.T, preferred_element_type=jnp.float32)
    local_gain = jnp.sum(grad_z * normed, 0)
    grad_norm = grad_z * norm_gain
    grad_field = cot.astype(jnp.float32) + rstd * (
        grad_norm - normed * jnp.mean(grad_norm * normed, -1, keepdims=True)
    )
    grad_field = grad_field.reshape(lon_cells, lat_cells, chans)
    for turn_index in range(STEPS):
        grad_field = grad_field + laplace(kappa * grad_field)
    grad_drift = grad_field.astype(jnp.bfloat16)
    parts = (weights[:, :, None] * grad_drift.reshape(cells, chans).astype(jnp.float32)).astype(
        jnp.bfloat16
    )
    count = lon_cells * lax.axis_size("lon")
    width = count * lat_cells
    local = shifted
    onehot = (local[:, :, None] == jnp.arange(width, dtype=jnp.int32)[None, None, :]).astype(
        jnp.bfloat16
    )
    term = jnp.einsum("ksr,ksc->rc", onehot, parts, preferred_element_type=jnp.float32)
    summed = lax.psum_scatter(
        term.reshape(count, lat_cells, chans).astype(jnp.bfloat16),
        "lon",
        scatter_dimension=0,
        tiled=True,
    )
    grad_inner, grad_outer, grad_gain = lax.psum(
        (local_inner, local_outer, local_gain), ("lon", "lat")
    )
    return (state_out, summed, grad_inner, grad_outer, grad_gain)


def solution(mesh):
    placed = (
        P("lon", "lat", None),
        P("lon", "lat", None),
        P(),
        P(),
        P(),
        P("lon", "lat"),
        P("lon", "lat"),
        P("lon", "lat"),
        P("lon", "lat"),
        P("lon", "lat"),
        P(),
    )
    return jax.shard_map(
        on_device,
        mesh=mesh,
        in_specs=placed,
        out_specs=(P("lon", "lat", None), P("lon", "lat", None), P(), P(), P()),
        check_vma=False,
    )
```

profile of v0, /device:TPU:0, one launch (start us, length us, event | category | flops | bytes accessed | tf_op | source)
XLA Modules:
  0.0 660.8 jit_solution(15575041906602351369)
XLA Ops:
  11.2 9.1 %select_reduce_fusion = f32[256,8192]{0,1:T(8,128)} fusion(f32[4,256]{1,0:T(4,128)S(1)} %pad_maximum_fusion, s32[4,256]{1,0:T(4,128)S(1)} %pad_add_fusion), kind=kLoop, calls=%fused_computation | loop fusion | flops 23068672 | bytes 8396800 | tf_op jit(solution)/shard_map/reduce_sum | solution.py:71
  20.3 182.2 %all-gather.2.cloned.1.call-done = bf16[512,16,512]{2,1,0:T(8,128)(2,1)} async-done(((bf16[16,16,512]{2,1,0:T(8,128)(2,1)}), bf16[512,16,512]{2,1,0:T(8,128)(2,1)}) %all-gather.2.cloned.1.call-update) | async-done | bytes 8388624 | tf_op jit(solution)/shard_map/all_gather | solution.py:67
  202.5 8.3 %fusion.4 = f32[256,512]{1,0:T(8,128)S(1)} fusion(bf16[8192,512]{1,0:T(8,128)(2,1)} %bitcast.34, f32[256,8192]{0,1:T(8,128)} %select_reduce_fusion), kind=kOutput, calls=%fused_computation.9 | convolution fusion | flops 2149580800 | bytes 17301504 | tf_op jit(solution)/shard_map/dot_general | solution.py:75
  210.8 2.3 copy-done.2
  213.0 2.4 fusion.8
  215.5 6.2 collective-permute-start.1
  221.8 1.3 collective-permute-start.2
  223.1 1.3 collective-permute-start.3
  224.5 4.6 collective-permute-done.3
  229.6 6.2 collective-permute-start.5
  235.9 5.5 collective-permute-start.6
  241.4 1.5 collective-permute-start.7
  242.9 1.6 collective-permute-done.7
  245.0 6.2 collective-permute-start.9
  251.3 5.5 collective-permute-start.10
  256.8 1.3 collective-permute-start.11
  258.2 1.8 collective-permute-done.11
  260.4 6.2 collective-permute-start.13
  266.7 5.5 collective-permute-start.14
  272.2 1.3 collective-permute-start.15
  273.5 1.8 collective-permute-done.15
  276.5 1.8 fusion.47
  278.3 1.8 fusion.7
  280.1 1.8 fusion.75
  281.9 1.1 multiply_reduce_fusion
  283.9 6.2 collective-permute-start.17
  290.2 5.5 collective-permute-start.18
  295.7 1.3 collective-permute-start.19
  297.9 1.0 collective-permute-done.19
  299.3 6.2 collective-permute-start.21
  305.6 5.5 collective-permute-start.22
  311.1 1.3 collective-permute-start.23
  312.5 1.8 collective-permute-done.23
  314.8 6.2 collective-permute-start.25
  321.0 5.6 collective-permute-start.26
  326.6 1.3 collective-permute-start.27
  328.0 1.7 collective-permute-done.27
  330.2 6.2 collective-permute-start.29
  336.5 5.4 collective-permute-start.30
  342.0 1.5 collective-permute-start.31
  343.6 1.6 collective-permute-done.31
  345.6 11.1 %bitcast_convert_fusion = bf16[8192,512]{1,0:T(8,128)(2,1)} fusion(s32[4,256]{1,0:T(4,128)S(1)} %pad_add_fusion, f32[256,512]{1,0:T(8,128)S(1)} %bitcast_convert_fusion.1, f32[4,256]{1,0:T(4,128)S(1)} %pad_maximum_fusion), kind=kOutput, calls=%fused_computation.3 | convolution fusion | flops 8603566080 | bytes 8921088 | tf_op jit(solution)/shard_map/ksr,ksc->rc/dot_general | solution.py:116
  357.3 66.7 %psum.23 = f32[512]{0:T(512)} all-reduce(f32[512]{0:T(512)S(1)} %copy-done.5), channel_id=1, replica_groups=mesh['lon'=32,'lat'=4] {'lon','lat'}, use_global_device_ids=true, to_apply=%region_8.9 | all-reduce | flops 512 | bytes 4096 | tf_op jit(solution)/shard_map/psum | solution.py:123
  424.0 2.4 fusion.9
  426.5 23.1 %all-reduce.3.cloned.1.call-done = (f32[512,1024]{1,0:T(8,128)}, f32[1024,512]{1,0:T(8,128)}) async-done(((f32[512,1024]{1,0:T(8,128)}, f32[1024,512]{1,0:T(8,128)}), (f32[512,1024]{1,0:T(8,128)}, f32[1024,512]{1,0:T(8,128)})) %all-reduce.3.cloned.1.call-update) | async-done | bytes 4194320 | tf_op jit(solution)/shard_map/psum | solution.py:123
  449.6 198.4 %reduce-scatter.2.cloned.1.call-done = bf16[16,16,512]{2,1,0:T(8,128)(2,1)} async-done(((bf16[512,16,512]{2,1,0:T(8,128)(2,1)}), bf16[16,16,512]{2,1,0:T(8,128)(2,1)}) %reduce-scatter.2.cloned.1.call-update) | async-done | bytes 262160 | tf_op jit(solution)/shard_map/reduce_scatter | solution.py:117
  648.0 3.2 copy.18
  651.2 3.1 copy.19
  (107 shorter events, 11.5 us)
Async XLA Ops:
  7.2 268.8 %copy-start = (bf16[512,1024]{1,0:T(8,128)(2,1)S(1)}, bf16[512,1024]{1,0:T(8,128)(2,1)}, u32[]{:S(2)}) copy-start(bf16[512,1024]{1,0:T(8,128)(2,1)} %param.13) | copy-start | bytes 3145732
  7.2 195.3 %all-gather.2.cloned.1.call-start = ((), (), s32[]{:S(2)}) async-start(), calls=%async_computation.1 | async-start | bytes 8650752 | tf_op jit(solution)/shard_map/all_gather | solution.py:67
  7.9 441.6 %all-reduce.3.cloned.1.call-start = ((), (), s32[]{:S(2)}) async-start(), calls=%async_computation.3 | async-start | bytes 8388608 | tf_op jit(solution)/shard_map/psum | solution.py:123
  202.5 8.3 %copy-start.1 = (f32[256,8192]{0,1:T(8,128)S(1)}, f32[256,8192]{0,1:T(8,128)}, u32[]{:S(2)}) copy-start(f32[256,8192]{0,1:T(8,128)} %select_reduce_fusion) | copy-start | bytes 25165828
  202.5 10.5 %copy-start.2 = (bf16[512,16,512]{2,1,0:T(8,128)(2,1)S(1)}, bf16[512,16,512]{2,1,0:T(8,128)(2,1)}, u32[]{:S(2)}) copy-start(bf16[512,16,512]{2,1,0:T(8,128)(2,1)} %all-gather.2.cloned.1.call-done) | copy-start | bytes 25165828
  215.4 9.0 %collective-permute-start = (bf16[1,16,512]{2,1,0:T(8,128)(2,1)S(1)}, bf16[1,16,512]{2,1,0:T(8,128)(2,1)S(1)}, u32[]{:S(2)}, u32[]{:S(2)}) collective-permute-start(bf16[1,16,512]{2,1,0:T(8,128)(2,1)S(1)} %get-tuple-element.51), channel_id=1, source_target_pairs={{0,4},{4,8},{8,12},{12,16},{16,20},{20,24},{24,28},{28,32},{32,36}... | collective-permute-start | bytes 49160 | tf_op jit(solution)/shard_map/ppermute | solution.py:16
  215.5 8.9 %collective-permute-start.1 = (bf16[1,16,512]{2,1,0:T(8,128)(2,1)S(1)}, bf16[1,16,512]{2,1,0:T(8,128)(2,1)S(1)}, u32[]{:S(2)}, u32[]{:S(2)}) collective-permute-start(bf16[1,16,512]{2,1,0:T(8,128)(2,1)S(1)} %get-tuple-element.52), channel_id=1, source_target_pairs={{4,0},{8,4},{12,8},{16,12},{20,16},{24,20},{28,24},{32,28},{36,32}... | collective-permute-start | bytes 49160 | tf_op jit(solution)/shard_map/ppermute | solution.py:17
  221.8 2.7 collective-permute-start.2
  223.1 6.0 collective-permute-start.3
  229.5 46.4 %copy-start.4 = (f32[512]{0:T(512)S(1)}, f32[512]{0:T(512)}, u32[]{:S(2)}) copy-start(f32[512]{0:T(512)} %param.15) | copy-start | bytes 6148
  229.5 13.3 %collective-permute-start.4 = (bf16[1,16,512]{2,1,0:T(8,128)(2,1)S(1)}, bf16[1,16,512]{2,1,0:T(8,128)(2,1)S(1)}, u32[]{:S(2)}, u32[]{:S(2)}) collective-permute-start(bf16[1,16,512]{2,1,0:T(8,128)(2,1)S(1)} %get-tuple-element.47), channel_id=1, source_target_pairs={{0,4},{4,8},{8,12},{12,16},{16,20},{20,24},{24,28},{28,32},{32,36}... | collective-permute-start | bytes 49160 | tf_op jit(solution)/shard_map/ppermute | solution.py:16
  229.6 13.3 %collective-permute-start.5 = (bf16[1,16,512]{2,1,0:T(8,128)(2,1)S(1)}, bf16[1,16,512]{2,1,0:T(8,128)(2,1)S(1)}, u32[]{:S(2)}, u32[]{:S(2)}) collective-permute-start(bf16[1,16,512]{2,1,0:T(8,128)(2,1)S(1)} %get-tuple-element.48), channel_id=1, source_target_pairs={{4,0},{8,4},{12,8},{16,12},{20,16},{24,20},{28,24},{32,28},{36,32}... | collective-permute-start | bytes 49160 | tf_op jit(solution)/shard_map/ppermute | solution.py:17
  235.9 7.1 %collective-permute-start.6 = (bf16[16,1,512]{2,1,0:T(2,128)(2,1)S(1)}, bf16[16,1,512]{2,1,0:T(2,128)(2,1)S(1)}, u32[]{:S(2)}, u32[]{:S(2)}) collective-permute-start(bf16[16,1,512]{2,1,0:T(2,128)(2,1)S(1)} %get-tuple-element.49), channel_id=1, source_target_pairs={{0,1},{1,2},{2,3},{4,5},{5,6},{6,7},{8,9},{9,10},{10,11},{12,13},{... | collective-permute-start | bytes 49160 | tf_op jit(solution)/shard_map/ppermute | solution.py:16
  241.4 3.2 collective-permute-start.7
  244.7 31.8 %copy-start.3 = (bf16[16,16,512]{2,1,0:T(8,128)(2,1)S(1)}, bf16[16,16,512]{2,1,0:T(8,128)(2,1)}, u32[]{:S(2)}) copy-start(bf16[16,16,512]{2,1,0:T(8,128)(2,1)} %param.12) | copy-start | bytes 786436
  244.9 13.2 %collective-permute-start.8 = (bf16[1,16,512]{2,1,0:T(8,128)(2,1)S(1)}, bf16[1,16,512]{2,1,0:T(8,128)(2,1)S(1)}, u32[]{:S(2)}, u32[]{:S(2)}) collective-permute-start(bf16[1,16,512]{2,1,0:T(8,128)(2,1)S(1)} %get-tuple-element.43), channel_id=1, source_target_pairs={{0,4},{4,8},{8,12},{12,16},{16,20},{20,24},{24,28},{28,32},{32,36}... | collective-permute-start | bytes 49160 | tf_op jit(solution)/shard_map/ppermute | solution.py:16
  245.0 13.1 %collective-permute-start.9 = (bf16[1,16,512]{2,1,0:T(8,128)(2,1)S(1)}, bf16[1,16,512]{2,1,0:T(8,128)(2,1)S(1)}, u32[]{:S(2)}, u32[]{:S(2)}) collective-permute-start(bf16[1,16,512]{2,1,0:T(8,128)(2,1)S(1)} %get-tuple-element.44), channel_id=1, source_target_pairs={{4,0},{8,4},{12,8},{16,12},{20,16},{24,20},{28,24},{32,28},{36,32}... | collective-permute-start | bytes 49160 | tf_op jit(solution)/shard_map/ppermute | solution.py:17
  251.3 6.9 %collective-permute-start.10 = (bf16[16,1,512]{2,1,0:T(2,128)(2,1)S(1)}, bf16[16,1,512]{2,1,0:T(2,128)(2,1)S(1)}, u32[]{:S(2)}, u32[]{:S(2)}) collective-permute-start(bf16[16,1,512]{2,1,0:T(2,128)(2,1)S(1)} %get-tuple-element.45), channel_id=1, source_target_pairs={{0,1},{1,2},{2,3},{4,5},{5,6},{6,7},{8,9},{9,10},{10,11},{12,13},{... | collective-permute-start | bytes 49160 | tf_op jit(solution)/shard_map/ppermute | solution.py:16
  256.8 3.2 collective-permute-start.11
  260.3 13.2 %collective-permute-start.12 = (bf16[1,16,512]{2,1,0:T(8,128)(2,1)S(1)}, bf16[1,16,512]{2,1,0:T(8,128)(2,1)S(1)}, u32[]{:S(2)}, u32[]{:S(2)}) collective-permute-start(bf16[1,16,512]{2,1,0:T(8,128)(2,1)S(1)} %get-tuple-element.39), channel_id=1, source_target_pairs={{0,4},{4,8},{8,12},{12,16},{16,20},{20,24},{24,28},{28,32},{32,36}... | collective-permute-start | bytes 49160 | tf_op jit(solution)/shard_map/ppermute | solution.py:16
  260.4 13.1 %collective-permute-start.13 = (bf16[1,16,512]{2,1,0:T(8,128)(2,1)S(1)}, bf16[1,16,512]{2,1,0:T(8,128)(2,1)S(1)}, u32[]{:S(2)}, u32[]{:S(2)}) collective-permute-start(bf16[1,16,512]{2,1,0:T(8,128)(2,1)S(1)} %get-tuple-element.40), channel_id=1, source_target_pairs={{4,0},{8,4},{12,8},{16,12},{20,16},{24,20},{28,24},{32,28},{36,32}... | collective-permute-start | bytes 49160 | tf_op jit(solution)/shard_map/ppermute | solution.py:17
  266.7 6.9 %collective-permute-start.14 = (bf16[16,1,512]{2,1,0:T(2,128)(2,1)S(1)}, bf16[16,1,512]{2,1,0:T(2,128)(2,1)S(1)}, u32[]{:S(2)}, u32[]{:S(2)}) collective-permute-start(bf16[16,1,512]{2,1,0:T(2,128)(2,1)S(1)} %get-tuple-element.41), channel_id=1, source_target_pairs={{0,1},{1,2},{2,3},{4,5},{5,6},{6,7},{8,9},{9,10},{10,11},{12,13},{... | collective-permute-start | bytes 49160 | tf_op jit(solution)/shard_map/ppermute | solution.py:16
  272.2 3.2 collective-permute-start.15
  283.9 13.2 %collective-permute-start.16 = (bf16[1,16,512]{2,1,0:T(8,128)(2,1)}, bf16[1,16,512]{2,1,0:T(8,128)(2,1)}, u32[]{:S(2)}, u32[]{:S(2)}) collective-permute-start(bf16[1,16,512]{2,1,0:T(8,128)(2,1)} %get-tuple-element.35), channel_id=1, source_target_pairs={{0,4},{4,8},{8,12},{12,16},{16,20},{20,24},{24,28},{28,32},{32,36}... | collective-permute-start | bytes 49160 | tf_op jit(solution)/shard_map/ppermute | solution.py:16
  283.9 13.2 %collective-permute-start.17 = (bf16[1,16,512]{2,1,0:T(8,128)(2,1)}, bf16[1,16,512]{2,1,0:T(8,128)(2,1)}, u32[]{:S(2)}, u32[]{:S(2)}) collective-permute-start(bf16[1,16,512]{2,1,0:T(8,128)(2,1)} %get-tuple-element.36), channel_id=1, source_target_pairs={{4,0},{8,4},{12,8},{16,12},{20,16},{24,20},{28,24},{32,28},{36,32}... | collective-permute-start | bytes 49160 | tf_op jit(solution)/shard_map/ppermute | solution.py:17
  290.2 7.7 %collective-permute-start.18 = (bf16[16,1,512]{2,1,0:T(2,128)(2,1)S(1)}, bf16[16,1,512]{2,1,0:T(2,128)(2,1)S(1)}, u32[]{:S(2)}, u32[]{:S(2)}) collective-permute-start(bf16[16,1,512]{2,1,0:T(2,128)(2,1)S(1)} %get-tuple-element.37), channel_id=1, source_target_pairs={{0,1},{1,2},{2,3},{4,5},{5,6},{6,7},{8,9},{9,10},{10,11},{12,13},{... | collective-permute-start | bytes 49160 | tf_op jit(solution)/shard_map/ppermute | solution.py:16
  295.7 3.2 collective-permute-start.19
  297.0 351.0 %reduce-scatter.2.cloned.1.call-start = ((), (), s32[]{:S(2)}) async-start(), calls=%async_computation.2 | async-start | bytes 8650752 | tf_op jit(solution)/shard_map/reduce_scatter | solution.py:117
  299.2 13.2 %collective-permute-start.20 = (bf16[1,16,512]{2,1,0:T(8,128)(2,1)S(1)}, bf16[1,16,512]{2,1,0:T(8,128)(2,1)S(1)}, u32[]{:S(2)}, u32[]{:S(2)}) collective-permute-start(bf16[1,16,512]{2,1,0:T(8,128)(2,1)S(1)} %get-tuple-element.31), channel_id=1, source_target_pairs={{0,4},{4,8},{8,12},{12,16},{16,20},{20,24},{24,28},{28,32},{32,36}... | collective-permute-start | bytes 49160 | tf_op jit(solution)/shard_map/ppermute | solution.py:16
  299.3 13.1 %collective-permute-start.21 = (bf16[1,16,512]{2,1,0:T(8,128)(2,1)S(1)}, bf16[1,16,512]{2,1,0:T(8,128)(2,1)S(1)}, u32[]{:S(2)}, u32[]{:S(2)}) collective-permute-start(bf16[1,16,512]{2,1,0:T(8,128)(2,1)S(1)} %get-tuple-element.32), channel_id=1, source_target_pairs={{4,0},{8,4},{12,8},{16,12},{20,16},{24,20},{28,24},{32,28},{36,32}... | collective-permute-start | bytes 49160 | tf_op jit(solution)/shard_map/ppermute | solution.py:17
  305.6 6.9 %collective-permute-start.22 = (bf16[16,1,512]{2,1,0:T(2,128)(2,1)S(1)}, bf16[16,1,512]{2,1,0:T(2,128)(2,1)S(1)}, u32[]{:S(2)}, u32[]{:S(2)}) collective-permute-start(bf16[16,1,512]{2,1,0:T(2,128)(2,1)S(1)} %get-tuple-element.33), channel_id=1, source_target_pairs={{0,1},{1,2},{2,3},{4,5},{5,6},{6,7},{8,9},{9,10},{10,11},{12,13},{... | collective-permute-start | bytes 49160 | tf_op jit(solution)/shard_map/ppermute | solution.py:16
  311.1 3.2 collective-permute-start.23
  314.7 13.3 %collective-permute-start.24 = (bf16[1,16,512]{2,1,0:T(8,128)(2,1)S(1)}, bf16[1,16,512]{2,1,0:T(8,128)(2,1)S(1)}, u32[]{:S(2)}, u32[]{:S(2)}) collective-permute-start(bf16[1,16,512]{2,1,0:T(8,128)(2,1)S(1)} %get-tuple-element.27), channel_id=1, source_target_pairs={{0,4},{4,8},{8,12},{12,16},{16,20},{20,24},{24,28},{28,32},{32,36}... | collective-permute-start | bytes 49160 | tf_op jit(solution)/shard_map/ppermute | solution.py:16
  314.8 13.2 %collective-permute-start.25 = (bf16[1,16,512]{2,1,0:T(8,128)(2,1)S(1)}, bf16[1,16,512]{2,1,0:T(8,128)(2,1)S(1)}, u32[]{:S(2)}, u32[]{:S(2)}) collective-permute-start(bf16[1,16,512]{2,1,0:T(8,128)(2,1)S(1)} %get-tuple-element.28), channel_id=1, source_target_pairs={{4,0},{8,4},{12,8},{16,12},{20,16},{24,20},{28,24},{32,28},{36,32}... | collective-permute-start | bytes 49160 | tf_op jit(solution)/shard_map/ppermute | solution.py:17
  321.0 7.0 %collective-permute-start.26 = (bf16[16,1,512]{2,1,0:T(2,128)(2,1)S(1)}, bf16[16,1,512]{2,1,0:T(2,128)(2,1)S(1)}, u32[]{:S(2)}, u32[]{:S(2)}) collective-permute-start(bf16[16,1,512]{2,1,0:T(2,128)(2,1)S(1)} %get-tuple-element.29), channel_id=1, source_target_pairs={{0,1},{1,2},{2,3},{4,5},{5,6},{6,7},{8,9},{9,10},{10,11},{12,13},{... | collective-permute-start | bytes 49160 | tf_op jit(solution)/shard_map/ppermute | solution.py:16
  326.6 3.1 collective-permute-start.27
  330.1 13.3 %collective-permute-start.28 = (bf16[1,16,512]{2,1,0:T(8,128)(2,1)S(1)}, bf16[1,16,512]{2,1,0:T(8,128)(2,1)S(1)}, u32[]{:S(2)}, u32[]{:S(2)}) collective-permute-start(bf16[1,16,512]{2,1,0:T(8,128)(2,1)S(1)} %get-tuple-element.23), channel_id=1, source_target_pairs={{0,4},{4,8},{8,12},{12,16},{16,20},{20,24},{24,28},{28,32},{32,36}... | collective-permute-start | bytes 49160 | tf_op jit(solution)/shard_map/ppermute | solution.py:16
  330.2 13.3 %collective-permute-start.29 = (bf16[1,16,512]{2,1,0:T(8,128)(2,1)S(1)}, bf16[1,16,512]{2,1,0:T(8,128)(2,1)S(1)}, u32[]{:S(2)}, u32[]{:S(2)}) collective-permute-start(bf16[1,16,512]{2,1,0:T(8,128)(2,1)S(1)} %get-tuple-element.24), channel_id=1, source_target_pairs={{4,0},{8,4},{12,8},{16,12},{20,16},{24,20},{28,24},{32,28},{36,32}... | collective-permute-start | bytes 49160 | tf_op jit(solution)/shard_map/ppermute | solution.py:17
  336.5 7.1 %collective-permute-start.30 = (bf16[16,1,512]{2,1,0:T(2,128)(2,1)S(1)}, bf16[16,1,512]{2,1,0:T(2,128)(2,1)S(1)}, u32[]{:S(2)}, u32[]{:S(2)}) collective-permute-start(bf16[16,1,512]{2,1,0:T(2,128)(2,1)S(1)} %get-tuple-element.25), channel_id=1, source_target_pairs={{0,1},{1,2},{2,3},{4,5},{5,6},{6,7},{8,9},{9,10},{10,11},{12,13},{... | collective-permute-start | bytes 49160 | tf_op jit(solution)/shard_map/ppermute | solution.py:16
  342.0 3.2 collective-permute-start.31
  356.6 0.7 copy-start.5
Sparse Core Ops, SparseCore 0:
  9.7 192.7 all-gather.1
  297.1 152.3 all-reduce.2
  452.5 195.4 reduce-scatter.1
where the time goes:
time: 662 us; the launch traced here: 661 us
  waiting for transfers between devices  420 us (63%)
  starting transfers between devices  101 us (15%)
  blocking collectives  66.7 us (10%)
  matrix products  31.1 us (5%)
  other arithmetic  15.2 us (2%)
  between operations  14.5 us (2%)
  local copies, waits for them, and re-layouts  12 us (2%)
    reduce_scatter x1, waiting for transfers between devices, on_device(): lax.psum_scatter(term.reshape(count, lat_cells, chans).astype(jnp.bfloat1...  198 us
    all_gather x1, waiting for transfers between devices, on_device(): shard_piece = lax.all_gather(latent_state, 'lon', axis=0, tiled=True)  182 us
    psum x1, blocking collectives, on_device(): lax.psum((local_inner, local_outer, local_gain), ('lon', 'lat'))  66.7 us
    ppermute x16, starting transfers between devices, with_halo(): after = lax.ppermute(first, axis, down)  60.6 us
    ppermute x16, starting transfers between devices, with_halo(): before = lax.ppermute(last, axis, up)  40.3 us
    psum x1, waiting for transfers between devices, on_device(): lax.psum((local_inner, local_outer, local_gain), ('lon', 'lat'))  23.1 us
    ppermute x16, waiting for transfers between devices, with_halo(): after = lax.ppermute(first, axis, down)  15.8 us
  transfers between devices with their start and end apart: 35, of which 11 were waited for; matrix products, arithmetic and copies ran while one was open for 4% of the time, Pallas kernels for 0%

commit v1 on v0

--- a/solution.py
+++ b/solution.py
@@ -1,7 +1,83 @@
+import functools
+
 import jax
 import jax.numpy as jnp
+import numpy as np
 from jax import lax
+from jax.experimental import pallas as pl
+from jax.experimental.pallas import tpu as pltpu
 from jax.sharding import PartitionSpec as P
+
+MESH = pl.DeviceIdType.MESH
+F32 = jnp.float32
+BF16 = jnp.bfloat16
+NL = 32
+NT = 4
+CELLS = 256
+CH = 512
+HID = 1024
+SLOT = 64
+NS = NL * SLOT
+PAIRS = NL // 2
+NEAR_PAIRS = 6
+CAP_NEAR = 48
+CAP_FAR = 32
+BACK = 5
+EXT = 640
+NEIGH = ((-1, 0), (1, 0), (0, -1), (0, 1), (-1, -1), (-1, 1), (1, -1), (1, 1))
+
+
+def ext_cells():
+    cells = [(x, y) for x in range(16) for y in range(16)]
+    low, mid, top = range(-4, 0), range(16), range(16, 20)
+    for dx, dy in NEIGH:
+        xs = (low, mid, top)[dx + 1]
+        ys = (low, mid, top)[dy + 1]
+        cells += [(x, y) for x in xs for y in ys]
+    return np.array(cells)
+
+
+def tables():
+    cells = ext_cells()
+    count = len(cells)
+    dist = np.abs(cells[:, None] - cells[None, :]).sum(-1)
+    adj = np.zeros((EXT, EXT), np.float32)
+    adj[:count, :count] = dist == 1
+    ys = np.full((EXT,), -1000.0, np.float32)
+    ys[:count] = cells[:, 1]
+    ycol = np.broadcast_to(ys[:, None], (EXT, 128))
+    yrow = np.broadcast_to(ys[None, :], (8, EXT))
+    sel = np.zeros((384, CELLS), np.float32)
+    at = 0
+    for dx, dy in NEIGH:
+        width = (4 if dx else 16) * (4 if dy else 16)
+        for q in range(width):
+            x, y = cells[256 + at + q]
+            sel[at + q, (x - 16 * dx) * 16 + (y - 16 * dy)] = 1.0
+        at += width
+    spread = (np.arange(256)[None, :] % 16 == np.arange(16)[:, None]).astype(np.float32)
+    return adj, ycol, yrow, sel, spread
+
+
+def nn(a, b):
+    return jnp.dot(a, b, preferred_element_type=F32)
+
+
+def nt(a, b):
+    return lax.dot_general(a, b, (((1,), (1,)), ((), ())), preferred_element_type=F32)
+
+
+def tn(a, b):
+    return lax.dot_general(a, b, (((0,), (0,)), ((), ())), preferred_element_type=F32)
+
+
+def split2(v):
+    hi = v.astype(BF16)
+    return hi, (v - hi.astype(F32)).astype(BF16)
+
+
+def iota(shape, dim):
+    return lax.broadcasted_iota(jnp.int32, shape, dim).astype(F32)
 
 STEPS = 4
 
@@ -45,7 +121,7 @@
     return wide[2:] + wide[:-2] + tall[:, 2:] + tall[:, :-2] - 4.0 * field
 
 
-def on_device(
+def on_device_general(
     latent_state,
     cotangent,
     w_inner,
@@ -126,6 +202,490 @@
     return (state_out, summed, grad_inner, grad_outer, grad_gain)
 
 
+def kernel(
+    lat_state, cot_ref, w_in, w_out, gain_ref, sb_ref, cc_ref, fa_ref, fb_ref, ter_ref, ktab,
+    adj_ref, ycol_ref, yrow_ref, sel_ref, spread_ref,
+    out_ref, grad_ref, gout, vec_ref,
+    G, W_hi, W_lo, rows_out, rows_in, gro, gin, req_out, req_in, t_out, t_in,
+    ext_f, ext_b, stage_f, stage_b, gd_ref, Mh, Ml, M2h, M2l, Ah, Al, Bh, Bl,
+    z_ref, act_ref, gp_ref, gbuf, sib_in, hsum, rs_in, xh_out, xh_in, v_out, v_lat, v_sum, v_lon,
+    s_req, r_req, s_row, r_row, s_gro, r_gro, s_ter, r_ter, s_hf, r_hf, s_hb, r_hb,
+    s_sib, r_sib, s_rs, r_rs, s_xh, r_xh, s_ag, r_ag, s_fin, r_fin, s_vl, r_vl, s_vn, r_vn,
+):
+    me = lax.axis_index("lon")
+    la = lax.axis_index("lat")
+    core = lax.rem(la, 2)
+    sib = la + 1 - 2 * core
+    opp = lax.rem(la + 2, NT)
+
+    def lon_at(d):
+        return lax.rem(me + d + 2 * NL, NL)
+
+    def lat_at(d):
+        return lax.rem(la + d + NT, NT)
+
+    def send(src, dst, ssem, rsem, lon, lat):
+        return pltpu.make_async_remote_copy(
+            src_ref=src, dst_ref=dst, send_sem=ssem, recv_sem=rsem,
+            device_id=(lon, lat), device_id_type=MESH,
+        )
+
+    rows_in[...] = jnp.zeros((NS, CH), BF16)
+    gin[...] = jnp.zeros((NS, CH), BF16)
+    ext_f[576:EXT, :] = jnp.zeros((EXT - 576, CH), BF16)
+    ext_b[576:EXT, :] = jnp.zeros((EXT - 576, CH), BF16)
+
+    barrier = pltpu.get_barrier_semaphore()
+
+    def greet(d, carry):
+        pl.semaphore_signal(barrier, inc=1, device_id=(lon_at(d), la), device_id_type=MESH)
+        return carry
+
+    lax.fori_loop(1, NL, greet, 0)
+    for dx, dy in NEIGH[2:]:
+        pl.semaphore_signal(
+            barrier, inc=1, device_id=(lon_at(dx), lat_at(dy)), device_id_type=MESH
+        )
+    pl.semaphore_signal(barrier, inc=1, device_id=(me, opp), device_id_type=MESH)
+
+    raw = jnp.concatenate(
+        [
+            sb_ref[...].astype(F32), cc_ref[...].astype(F32), fa_ref[...], fb_ref[...],
+            ter_ref[...].astype(F32),
+        ],
+        axis=0,
+    )
+    flat = jnp.dot(
+        raw, spread_ref[...], precision=lax.Precision.HIGHEST, preferred_element_type=F32
+    )
+    own = jnp.floor(iota((16, CELLS), 1) * (1.0 / 16.0)) == iota((16, CELLS), 0)
+
+    def line(k):
+        return jnp.sum(jnp.where(own, flat[16 * k : 16 * k + 16], 0.0), 0, keepdims=True)
+
+    sb, cc, fa, fb, ter = (line(k) for k in range(5))
+    dev = jnp.floor(sb * 0.25)
+    blon = jnp.floor(sb * 0.5)
+    klon = jnp.floor(cc * 0.125)
+    cell = ((blon - 2.0 * dev) * 8.0 + klon) * 16.0 + (sb - 2.0 * blon) * 8.0 + (cc - 8.0 * klon)
+    slot = dev - me.astype(F32) + float(BACK)
+    slot = jnp.where(slot < 0.0, slot + float(NL), slot)
+    slot = jnp.where(slot >= float(NL), slot - float(NL), slot)
+    hits = iota((NL, CELLS), 0) == slot
+    before = (iota((CELLS, CELLS), 0) < iota((CELLS, CELLS), 1)).astype(F32).astype(BF16)
+    counts = nn(jnp.where(hits, 1.0, 0.0).astype(BF16), before)
+    rank = jnp.sum(jnp.where(hits, counts, 0.0), 0, keepdims=True)
+    cap = jnp.where(slot < 2.0 * NEAR_PAIRS, float(CAP_NEAR), float(CAP_FAR))
+    fits = rank < cap
+    place = jnp.where(fits, slot * float(SLOT) + rank, -1.0)
+    over = jnp.sum(jnp.where(fits, 0.0, 1.0), axis=1, keepdims=True)
+
+    def fill_g(q, carry):
+        row = pl.multiple_of(q * 128, 128)
+        at = iota((128, CELLS), 0) + lax.convert_element_type(row, F32)
+        G[pl.ds(row, 128), :] = jnp.where(at == place, 1.0, 0.0).astype(BF16)
+        return carry
+
+    lax.fori_loop(0, PAIRS, fill_g, 0)
+
+    def rows_of(lines, height, width):
+        which = iota((height, width), 0)
+        out = jnp.zeros((height, width), F32)
+        for k, v in enumerate(lines):
+            out = out + jnp.where(which == float(k), v, 0.0)
+        return out
+
+    fah = fa.astype(BF16).astype(F32)
+    fam = (fa - fah).astype(BF16).astype(F32)
+    fbh = fb.astype(BF16).astype(F32)
+    fbm = (fb - fbh).astype(BF16).astype(F32)
+    params = rows_of(
+        [cell, fah, fam, fa - fah - fam, fbh, fbm, fb - fbh - fbm, jnp.ones_like(fa)], 16, CELLS
+    ).astype(BF16)
+    for p in range(PAIRS):
+        req_out[p] = nt(params, G[128 * p : 128 * p + 128, :])[0:8]
+    t_all = nt(jnp.broadcast_to(ter, (16, CELLS)).astype(BF16), sel_ref[...])
+    for q in range(3):
+        t_out[q] = t_all[0:8, 128 * q : 128 * q + 128]
+
+    pl.semaphore_wait(barrier, NL - 1 + 7)
+
+    def req_copy(j):
+        return send(
+            req_out.at[j // 2], req_in.at[j], s_req.at[j], r_req.at[j], lon_at(j - BACK), la
+        )
+
+    def each_pair(body):
+        def step(j, carry):
+            @pl.when(j != BACK)
+            def _():
+                body(j)
+
+            return carry
+
+        lax.fori_loop(0, NL, step, 0)
+
+    each_pair(lambda j: req_copy(j).start())
+
+    def ter_copy(n):
+        dx, dy = NEIGH[n]
+        tile = (0, 0, 1, 1, 2, 2, 2, 2)[n]
+        return send(
+            t_out.at[tile], t_in.at[n], s_ter.at[n], r_ter.at[n], lon_at(-dx), lat_at(-dy)
+        )
+
+    for n in range(8):
+        ter_copy(n).start()
+    req_in[BACK] = req_out[BACK // 2]
+
+    each_pair(lambda j: req_copy(j).wait_recv())
+    lane_low = iota((8, 128), 1) < float(SLOT)
+
+    def row_copy(j, cap_j):
+        at = pl.multiple_of(j * SLOT, SLOT)
+        return send(
+            rows_out.at[pl.ds(at, cap_j), :], rows_in.at[pl.ds(at, cap_j), :],
+            s_row.at[j], r_row.at[j], lon_at(BACK - j), la,
+        )
+
+    def make_rows(cap_j):
+        def body(p, carry):
+            t = jnp.where(lane_low, req_in[2 * p], req_in[2 * p + 1])
+            cid = t[0:1]
+            a = t[1:2] + t[2:3] + t[3:4]
+            b = t[4:5] + t[5:6] + t[6:7]
+            real = t[7:8]
+            at = iota((CELLS, 128), 0) - cid
+            w = (
+                jnp.where(at == 0.0, (1.0 - a) * (1.0 - b) * real, 0.0)
+                + jnp.where(at == 16.0, a * (1.0 - b) * real, 0.0)
+                + jnp.where(at == 1.0, (1.0 - a) * b * real, 0.0)
+                + jnp.where(at == 17.0, a * b * real, 0.0)
+            )
+            hi, lo = split2(w)
+            col = pl.multiple_of(p * 128, 128)
+            W_hi[:, pl.ds(col, 128)] = hi
+            W_lo[:, pl.ds(col, 128)] = lo
+            v = lat_state[...]
+            rows_out[pl.ds(col, 128), :] = (tn(hi, v) + tn(lo, v)).astype(BF16)
+            for j in (2 * p, 2 * p + 1):
+                @pl.when(j != BACK)
+                def _():
+                    row_copy(j, cap_j).start()
+
+            return carry
+
+        return body
+
+    lax.fori_loop(0, NEAR_PAIRS, make_rows(CAP_NEAR), 0)
+    lax.fori_loop(NEAR_PAIRS, PAIRS, make_rows(CAP_FAR), 0)
+    own_rows = slice(BACK * SLOT, BACK * SLOT + SLOT)
+    rows_in[own_rows, :] = rows_out[own_rows, :]
+
+    for n in range(8):
+        ter_copy(n).wait_recv()
+    lane = iota((8, 128), 1)
+    quarter = jnp.floor(lane * (1.0 / 16.0))
+    corner = t_in[4]
+    for k in range(1, 4):
+        corner = jnp.where(quarter == float(k), t_in[4 + k], corner)
+    t_ext = jnp.concatenate(
+        [
+            jnp.broadcast_to(ter, (8, CELLS)),
+            jnp.where(lane_low, t_in[0], t_in[1]),
+            jnp.where(lane_low, t_in[2], t_in[3]),
+            corner,
+        ],
+        axis=1,
+    )
+    lat0 = (la * 16).astype(F32)
+    yr = yrow_ref[...] + lat0
+    kap = jnp.zeros((8, EXT), F32)
+    for k in range(8):
+        kap = kap + jnp.where(t_ext == float(k), ktab[k], 0.0)
+    kap = jnp.where((yr >= 0.0) & (yr < 64.0), kap, 0.0)[0:1]
+    for q in range(EXT // 128):
+        block = slice(128 * q, 128 * q + 128)
+        eye = iota((128, EXT), 0) + float(128 * q) == iota((128, EXT), 1)
+        m = adj_ref[block, :].astype(F32) * kap + jnp.where(eye, 1.0 - 4.0 * kap, 0.0)
+        yc = ycol_ref[block, 0:1].astype(F32) + lat0
+        m = jnp.where((yc >= 0.0) & (yc < 64.0), m, 0.0)
+        Mh[block, :], Ml[block, :] = split2(m)
+
+    def prod(ah, al, bh, bl):
+        return nn(ah, bh) + (nn(ah, bl) + nn(al, bh))
+
+    for q in range(EXT // 128):
+        block = slice(128 * q, 128 * q + 128)
+        m2 = prod(Mh[block, :], Ml[block, :], Mh[...], Ml[...])
+        M2h[block, :], M2l[block, :] = split2(m2)
+    for q in range(EXT // 128):
+        block = slice(128 * q, 128 * q + 128)
+        v = prod(M2h[block, :], M2l[block, :], M2h[:, 0:CELLS], M2l[:, 0:CELLS])
+        Ah[block, :], Al[block, :] = split2(v)
+    for q in range(CELLS // 128):
+        block = slice(128 * q, 128 * q + 128)
+        v = prod(M2h[block, :], M2l[block, :], M2h[...], M2l[...])
+        Bh[block, :], Bl[block, :] = split2(v)
+
+    def both_caps(body):
+        def near(j, carry):
+            @pl.when(j != BACK)
+            def _():
+                body(j, CAP_NEAR)
+
+            return carry
+
+        def far(j, carry):
+            body(j, CAP_FAR)
+            return carry
+
+        lax.fori_loop(0, 2 * NEAR_PAIRS, near, 0)
+        lax.fori_loop(2 * NEAR_PAIRS, NL, far, 0)
+
+    both_caps(lambda j, c: row_copy(j, c).wait_recv())
+    ext_f[0:CELLS, :] = tn(G[...], rows_in[...]).astype(BF16)
+
+    def halo_copy(ext, stage, ssem, rsem, n):
+        dx, dy = NEIGH[n]
+        start = (256, 320, 384, 448, 512, 528, 544, 560)[n]
+        size = 64 if n < 4 else 16
+        if n == 0:
+            src = ext.at[192:256, :]
+        elif n == 1:
+            src = ext.at[0:64, :]
+        else:
+            src = stage.at[start - 384 : start - 384 + size, :]
+        return send(
+            src, ext.at[start : start + size, :], ssem.at[n], rsem.at[n], lon_at(-dx), lat_at(-dy)
+        )
+
+    def halo_start(ext, stage, ssem, rsem):
+        for n in range(2):
+            halo_copy(ext, stage, ssem, rsem, n).start()
+        stage[...] = nn(sel_ref[128:320, :], ext[0:CELLS, :]).astype(BF16)
+        for n in range(2, 8):
+            halo_copy(ext, stage, ssem, rsem, n).start()
+
+    halo_start(ext_f, stage_f, s_hf, r_hf)
+    for n in range(8):
+        halo_copy(ext_f, stage_f, s_hf, r_hf, n).wait_recv()
+    field = tn(Ah[...], ext_f[...]) + tn(Al[...], ext_f[...])
+
+    gain = gain_ref[...]
+    r = lax.rsqrt(jnp.mean(field * field, axis=1, keepdims=True) + 1e-06)
+    normed = field * r
+    z = (normed * gain).astype(BF16)
+    z_ref[...] = z
+    cot = cot_ref[...]
+    react = jnp.zeros((CELLS, CH), F32)
+    gz = jnp.zeros((CELLS, CH), F32)
+    for h in range(4):
+        part = slice(256 * h, 256 * h + 256)
+        p = nn(z, w_in[:, part])
+        sig = 1.0 / (1.0 + jnp.exp(-p))
+        act = (p * sig).astype(BF16)
+        act_ref[:, part] = act
+        react = react + nn(act, w_out[part, :])
+        ga = nt(cot, w_out[part, :])
+        gp = (ga * sig * (1.0 + p * (1.0 - sig))).astype(BF16)
+        gp_ref[:, part] = gp
+        gz = gz + nt(gp, w_in[:, part])
+    out_ref[...] = (field + react).astype(BF16)
+    ggain = jnp.sum(gz * normed, axis=0, keepdims=True)
+    gn = gz * gain
+    gfield = cot.astype(F32) + r * (gn - normed * jnp.mean(gn * normed, axis=1, keepdims=True))
+    g_hi, g_lo = split2(gfield)
+    ext_b[0:CELLS, :] = g_hi
+    halo_start(ext_b, stage_b, s_hb, r_hb)
+
+    for h in range(2):
+        half = slice(512 * h, 512 * h + 512)
+        gbuf[h, 0] = tn(z_ref[...], gp_ref[:, half]).astype(BF16)
+        gbuf[h, 1] = tn(act_ref[:, half], cot_ref[...]).astype(BF16)
+    sib_copy = send(gbuf.at[1 - core], sib_in, s_sib, r_sib, me, sib)
+    sib_copy.start()
+    v_out[...] = rows_of(
+        [ggain[:, 128 * k : 128 * k + 128] for k in range(4)] + [jnp.broadcast_to(over, (1, 128))],
+        8, 128,
+    )
+
+    def vl_copy(d):
+        return send(v_out, v_lat.at[la], s_vl.at[d], r_vl.at[d], me, lat_at(d))
+
+    for d in range(1, NT):
+        vl_copy(d).start()
+    v_lat[pl.ds(la, 1)] = v_out[...].reshape(1, 8, 128)
+
+    for n in range(8):
+        halo_copy(ext_b, stage_b, s_hb, r_hb, n).wait_recv()
+    gdrift = (
+        nn(Bh[...], ext_b[...]) + nn(Bl[...], ext_b[...]) + nn(Bh[:, 0:CELLS], g_lo)
+    ).astype(BF16)
+
+    def gro_copy(j, cap_j):
+        at = pl.multiple_of(j * SLOT, SLOT)
+        return send(
+            gro.at[pl.ds(at, cap_j), :], gin.at[pl.ds(at, cap_j), :],
+            s_gro.at[j], r_gro.at[j], lon_at(j - BACK), la,
+        )
+
+    def bucket(cap_j):
+        def body(p, carry):
+            row = pl.multiple_of(p * 128, 128)
+            gro[pl.ds(row, 128), :] = nn(G[pl.ds(row, 128), :], gd_ref[...]).astype(BF16)
+            for j in (2 * p, 2 * p + 1):
+                @pl.when(j != BACK)
+                def _():
+                    gro_copy(j, cap_j).start()
+
+            return carry
+
+        return body
+
+    gd_ref[...] = gdrift
+    lax.fori_loop(0, NEAR_PAIRS, bucket(CAP_NEAR), 0)
+    lax.fori_loop(NEAR_PAIRS, PAIRS, bucket(CAP_FAR), 0)
+    gin[own_rows, :] = gro[own_rows, :]
+
+    sib_copy.wait_recv()
+    for k in range(2):
+        hsum[k] = (gbuf[core, k].astype(F32) + sib_in[k].astype(F32)).astype(BF16)
+
+    def rs_copy(d):
+        to = lon_at(d)
+        return send(
+            hsum.at[:, pl.ds(pl.multiple_of(to * 16, 16), 16), :], rs_in.at[d],
+            s_rs.at[d], r_rs.at[d], to, la,
+        )
+
+    def each_other(body):
+        def step(d, carry):
+            body(d)
+            return carry
+
+        lax.fori_loop(1, NL, step, 0)
+
+    each_other(lambda d: rs_copy(d).start())
+    mine = pl.ds(pl.multiple_of(me * 16, 16), 16)
+    rs_in[0] = hsum[:, mine, :]
+
+    for d in range(1, NT):
+        vl_copy(d).wait_recv()
+    v_sum[...] = v_lat[0] + v_lat[1] + v_lat[2] + v_lat[3]
+
+    def vn_copy(d):
+        return send(v_sum, v_lon.at[me], s_vn.at[d], r_vn.at[d], lon_at(d), la)
+
+    each_other(lambda d: vn_copy(d).start())
+    v_lon[pl.ds(me, 1)] = v_sum[...].reshape(1, 8, 128)
+
+    both_caps(lambda j, c: gro_copy(j, c).wait_recv())
+    grad_ref[...] = (nn(W_hi[...], gin[...]) + nn(W_lo[...], gin[...])).astype(BF16)
+
+    each_other(lambda d: rs_copy(d).wait_recv())
+    acc = jnp.zeros((2, 16, CH), F32)
+    for d in range(NL):
+        acc = acc + rs_in[d].astype(F32)
+    xh_out[...] = acc
+    xh_copy = send(xh_out, xh_in, s_xh, r_xh, me, opp)
+    xh_copy.start()
+    xh_copy.wait_recv()
+    gout[core, :, mine, :] = (xh_out[...] + xh_in[...]).astype(BF16)
+
+    def ag_copy(d):
+        piece = gout.at[core, :, mine, :]
+        return send(piece, piece, s_ag.at[d], r_ag.at[d], lon_at(d), la)
+
+    each_other(lambda d: ag_copy(d).start())
+    each_other(lambda d: vn_copy(d).wait_recv())
+    total = v_lon[0]
+    for k in range(1, NL):
+        total = total + v_lon[k]
+    vec_ref[...] = total
+    each_other(lambda d: ag_copy(d).wait_recv())
+    fin = send(gout.at[core], gout.at[core], s_fin, r_fin, me, sib)
+    fin.start()
+
+    each_pair(lambda j: req_copy(j).wait_send())
+    for n in range(8):
+        ter_copy(n).wait_send()
+        halo_copy(ext_f, stage_f, s_hf, r_hf, n).wait_send()
+        halo_copy(ext_b, stage_b, s_hb, r_hb, n).wait_send()
+    both_caps(lambda j, c: row_copy(j, c).wait_send())
+    both_caps(lambda j, c: gro_copy(j, c).wait_send())
+    sib_copy.wait_send()
+    for d in range(1, NT):
+        vl_copy(d).wait_send()
+    each_other(lambda d: rs_copy(d).wait_send())
+    each_other(lambda d: vn_copy(d).wait_send())
+    xh_copy.wait_send()
+    each_other(lambda d: ag_copy(d).wait_send())
+    fin.wait()
+
+
+def step_kernel(state, cot, w_in, w_out, gain, sb, cc, fa, fb, ter, ktab):
+    adj, ycol, yrow, sel, spread = tables()
+    vm = lambda *s, t=BF16: pltpu.VMEM(s, t)
+    dma = lambda *s: pltpu.SemaphoreType.DMA(s)
+    one = pltpu.SemaphoreType.DMA
+    scratch = [
+        vm(NS, CELLS), vm(CELLS, NS), vm(CELLS, NS), vm(NS, CH), vm(NS, CH), vm(NS, CH), vm(NS, CH),
+        vm(PAIRS, 8, 128, t=F32), vm(NL, 8, 128, t=F32), vm(3, 8, 128, t=F32), vm(8, 8, 128, t=F32),
+        vm(EXT, CH), vm(EXT, CH), vm(192, CH), vm(192, CH), vm(CELLS, CH),
+        vm(EXT, EXT), vm(EXT, EXT), vm(EXT, EXT), vm(EXT, EXT),
+        vm(EXT, CELLS), vm(EXT, CELLS), vm(CELLS, EXT), vm(CELLS, EXT),
+        vm(CELLS, CH), vm(CELLS, HID), vm(CELLS, HID),
+        vm(2, 2, 512, 512), vm(2, 512, 512), vm(2, 512, 512), vm(NL, 2, 16, 512),
+        vm(2, 16, 512, t=F32), vm(2, 16, 512, t=F32),
+        vm(8, 128, t=F32), vm(NT, 8, 128, t=F32), vm(8, 128, t=F32), vm(NL, 8, 128, t=F32),
+        dma(NL), dma(NL), dma(NL), dma(NL), dma(NL), dma(NL), dma(8), dma(8), dma(8), dma(8),
+        dma(8), dma(8), one, one, dma(NL), dma(NL), one, one, dma(NL), dma(NL), one, one,
+        dma(NT), dma(NT), dma(NL), dma(NL),
+    ]
+    vmem = pl.BlockSpec(memory_space=pltpu.VMEM)
+    smem = pl.BlockSpec(memory_space=pltpu.SMEM)
+    return pl.pallas_call(
+        kernel,
+        out_shape=(
+            jax.ShapeDtypeStruct((CELLS, CH), BF16),
+            jax.ShapeDtypeStruct((CELLS, CH), BF16),
+            jax.ShapeDtypeStruct((2, 2, 512, 512), BF16),
+            jax.ShapeDtypeStruct((8, 128), F32),
+        ),
+        in_specs=[vmem] * 10 + [smem] + [vmem] * 5,
+        out_specs=(vmem,) * 4,
+        scratch_shapes=scratch,
+        compiler_params=pltpu.CompilerParams(
+            collective_id=0, has_side_effects=True, vmem_limit_bytes=60 * 1024 * 1024
+        ),
+        cost_estimate=pl.CostEstimate(
+            flops=12 * 10**9, bytes_accessed=8 * 2**20, transcendentals=CELLS * HID
+        ),
+    )(
+        state, cot, w_in, w_out, gain.reshape(1, CH), sb, cc, fa, fb, ter, ktab,
+        jnp.asarray(adj, BF16), jnp.asarray(ycol, BF16), jnp.asarray(yrow, F32),
+        jnp.asarray(sel, BF16), jnp.asarray(spread, F32),
+    )
+
+
+def on_device(*args):
+    state, cot = (v.reshape(CELLS, CH) for v in args[:2])
+    state_out, state_grad, grads, vec = step_kernel(state, cot, *args[2:])
+    over = vec[4, 0]
+
+    def fast(state_out, state_grad, grads, vec, *rest):
+        inner = grads[:, 0].transpose(1, 0, 2).reshape(CH, HID).astype(F32)
+        outer = grads[:, 1].reshape(HID, CH).astype(F32)
+        shape = (16, 16, CH)
+        return state_out.reshape(shape), state_grad.reshape(shape), inner, outer, vec[0:4].reshape(CH)
+
+    def general(state_out, state_grad, grads, vec, *rest):
+        return on_device_general(*rest)
+
+    return lax.cond(over > 0.0, general, fast, state_out, state_grad, grads, vec, *args)
+
+
 def solution(mesh):
     placed = (
         P("lon", "lat", None),

time: 662 us -> 138 us (0.21)
  waiting for transfers between devices: 420 us -> 0 us
  Pallas kernels: 0 us -> 107 us
  starting transfers between devices: 101 us -> 0 us
  blocking collectives: 66.7 us -> 0 us
  matrix products: 31.1 us -> 0 us
  other arithmetic: 15.2 us -> 2.13 us
    reduce_scatter x1 -> x0, waiting for transfers between devices: 198 us -> none  [on_device(): lax.psum_scatter(term.reshape(count, lat_cells, chans).astype(jnp.bfloat1...]
    all_gather x1 -> x0, waiting for transfers between devices: 182 us -> none  [on_device(): shard_piece = lax.all_gather(latent_state, 'lon', axis=0, tiled=True)]
    pallas_call x0 -> x1, Pallas kernels: none -> 107 us  [step_kernel(): pl.pallas_call(kernel, out_shape=(jax.ShapeDtypeStruct((CELLS, CH), BF16)...]
    ppermute x32 -> x0, starting transfers between devices: 101 us -> none  [the longest x16 60.6 us: with_halo(): after = lax.ppermute(first, axis, down)]
    psum x1 -> x0, blocking collectives: 66.7 us -> none  [on_device(): lax.psum((local_inner, local_outer, local_gain), ('lon', 'lat'))]
    dot_general x9 -> x0, matrix products: 31.1 us -> none  [the longest x1 11.1 us: on_device(): jnp.einsum('ksr,ksc->rc', onehot, parts, preferred_element_type=jnp.float32)]
    psum x1 -> x0, waiting for transfers between devices: 23.1 us -> none  [on_device(): lax.psum((local_inner, local_outer, local_gain), ('lon', 'lat'))]
    ppermute x32 -> x0, waiting for transfers between devices: 15.9 us -> none  [the longest x16 15.8 us: with_halo(): after = lax.ppermute(first, axis, down)]
  transfers between devices with their start and end apart: 35 -> 0, of which waited for: 11 -> 0; matrix products, arithmetic and copies ran while one was open for 4% -> 0% of each run, Pallas kernels for 0% -> 0%
where the time goes in v1:
time: 138 us; the launch traced here: 136 us
  Pallas kernels  107 us (78%)
  between operations  14.8 us (11%)
  local copies, waits for them, and re-layouts  12.9 us (9%)
  other arithmetic  2.13 us (2%)
    pallas_call x1, Pallas kernels, step_kernel(): pl.pallas_call(kernel, out_shape=(jax.ShapeDtypeStruct((CELLS, CH), BF16)...  107 us
    unnamed x24, local copies, waits for them, and re-layouts  9.63 us

profile of v1, /device:TPU:0, one launch (start us, length us, event | category | flops | bytes accessed | tf_op | source)
XLA Modules:
  0.0 136.4 jit_solution(6010847088719110955)
XLA Ops:
  7.2 1.3 jit_solution_.3.yrow_ref
  8.5 0.0 copy-start.2
  8.5 0.0 copy-start.3
  8.5 0.0 copy-start.4
  8.5 0.0 copy-start.5
  8.5 0.0 copy-start.6
  8.5 0.0 copy-start.7
  8.5 0.0 copy-start.8
  8.5 0.0 copy-start.9
  8.5 0.0 copy-start.11
  8.5 106.6 %shard_map.201 = (bf16[256,512]{1,0:T(8,128)(2,1)}, bf16[256,512]{1,0:T(8,128)(2,1)}, bf16[2,2,512,512]{3,2,1,0:T(8,128)(2,1)S(1)}, f32[8,128]{1,0:T(8,128)S(1)}) custom-call(bf16[256,512]{1,0:T(8,128)(2,1)} %bitcast.63, bf16[256,512]{1,0:T(8,128)(2,1)} %bitcast.60, bf16[512,1024]{1,0:T(8,128)(2,1)} %w_in.1, bf16[1024,512]{1,0:T(8,128)(2,1)} %w_out.1, ...), custom_call_target="tpu_custom_call" | custom-call | flops 12000000000 | bytes 8388608 | tf_op jit(solution)/shard_map/pallas_call | solution.py:648
  115.1 0.5 slice.204
  116.3 0.0 copy-done.2
  116.3 0.0 copy-done.3
  116.3 0.0 copy-done.4
  116.3 0.0 copy-done.5
  116.3 0.0 copy-done.6
  116.3 0.0 copy-done.7
  116.3 0.0 copy-done.8
  116.3 0.0 copy-done.9
  116.4 0.0 copy-done.11
  116.4 3.6 %conditional.1 = (bf16[16,16,512]{2,1,0:T(8,128)(2,1)}, bf16[16,16,512]{2,1,0:T(8,128)(2,1)}, f32[512,1024]{1,0:T(8,128)}, f32[1024,512]{1,0:T(8,128)}, f32[512]{0:T(512)S(1)}) conditional(s32[]{:T(128)} %bitcast.18, (bf16[256,512]{1,0:T(8,128)(2,1)}, bf16[256,512]{1,0:T(8,128)(2,1)}, bf16[2,2,512,512]{3,2,1,0:T(8,128)(2,1)S(1)}, ...), branch_computations={%region_0.0_spmd, %region_1.11_spmd} | conditional | flops 14571300864 | bytes 266689824 | solution.py:686
  116.4 0.3 fusion.58
  116.7 1.5 %copy.34 = f32[2,64,8,512]{3,2,0,1:T(8,128)} copy(f32[2,64,8,512]{3,2,1,0:T(8,128)S(1)} %get-tuple-element.76) | data formatting | bytes 4194304 | tf_op jit(solution)/shard_map/cond/branch_0_fun/convert_element_type | solution.py:678
  118.2 1.8 %bitcast_convert_fusion = f32[1024,512]{1,0:T(8,128)} fusion(bf16[2,1,512,512]{3,2,1,0:T(8,128)(2,1)S(1)} %get-tuple-element.75), kind=kLoop, calls=%fused_computation.1 | loop fusion | flops 524288 | bytes 3145728 | tf_op jit(solution)/shard_map/cond/branch_0_fun/convert_element_type | solution.py:679
  120.0 0.0 copy-start.10
  120.0 1.7 %copy.49 = bf16[16,16,512]{2,1,0:T(8,128)(2,1)} copy(bf16[16,16,512]{2,1,0:T(8,128)(2,1)} %get-tuple-element.131) | data formatting | bytes 524288
  121.7 1.7 %copy.50 = bf16[16,16,512]{2,1,0:T(8,128)(2,1)} copy(bf16[16,16,512]{2,1,0:T(8,128)(2,1)} %get-tuple-element.132) | data formatting | bytes 524288
  123.3 3.2 %copy.51 = f32[512,1024]{1,0:T(8,128)} copy(f32[512,1024]{1,0:T(8,128)} %get-tuple-element.133) | data formatting | bytes 4194304
  126.5 3.1 %copy.52 = f32[1024,512]{1,0:T(8,128)} copy(f32[1024,512]{1,0:T(8,128)} %get-tuple-element.134) | data formatting | bytes 4194304
  129.6 0.0 copy-done.10
  (1 shorter events, 0.0 us)
Async XLA Ops:
  8.5 107.8 %copy-start.2 = (bf16[512,1024]{1,0:T(8,128)(2,1)S(1)}, bf16[512,1024]{1,0:T(8,128)(2,1)}, u32[]{:S(2)}) copy-start(bf16[512,1024]{1,0:T(8,128)(2,1)} %w_in.1) | copy-start | bytes 3145732
  8.5 107.8 %copy-start.3 = (bf16[16,16,512]{2,1,0:T(8,128)(2,1)S(1)}, bf16[16,16,512]{2,1,0:T(8,128)(2,1)}, u32[]{:S(2)}) copy-start(bf16[16,16,512]{2,1,0:T(8,128)(2,1)} %param.19) | copy-start | bytes 786436
  8.5 107.8 %copy-start.4 = (f32[512]{0:T(512)S(1)}, f32[512]{0:T(512)}, u32[]{:S(2)}) copy-start(f32[512]{0:T(512)} %param.22) | copy-start | bytes 6148
  8.5 107.8 %copy-start.5 = (s32[16,16]{1,0:T(8,128)S(1)}, s32[16,16]{1,0:T(8,128)}, u32[]{:S(2)}) copy-start(s32[16,16]{1,0:T(8,128)} %sb_ref.1) | copy-start | bytes 3076
  8.5 107.8 %copy-start.6 = (s32[16,16]{1,0:T(8,128)S(1)}, s32[16,16]{1,0:T(8,128)}, u32[]{:S(2)}) copy-start(s32[16,16]{1,0:T(8,128)} %cc_ref.1) | copy-start | bytes 3076
  8.5 107.8 %copy-start.7 = (f32[16,16]{1,0:T(8,128)S(1)}, f32[16,16]{1,0:T(8,128)}, u32[]{:S(2)}) copy-start(f32[16,16]{1,0:T(8,128)} %fa_ref.1) | copy-start | bytes 3076
  8.5 107.8 %copy-start.8 = (f32[16,16]{1,0:T(8,128)S(1)}, f32[16,16]{1,0:T(8,128)}, u32[]{:S(2)}) copy-start(f32[16,16]{1,0:T(8,128)} %fb_ref.1) | copy-start | bytes 3076
  8.5 107.8 %copy-start.9 = (s32[16,16]{1,0:T(8,128)S(1)}, s32[16,16]{1,0:T(8,128)}, u32[]{:S(2)}) copy-start(s32[16,16]{1,0:T(8,128)} %ter_ref.1) | copy-start | bytes 3076
  8.5 107.8 %copy-start.11 = (f32[8]{0:T(128)S(1)}, f32[8]{0:T(128)}, u32[]{:S(2)}) copy-start(f32[8]{0:T(128)} %ktab.1) | copy-start | bytes 100
  120.0 9.6 %copy-start.10 = (f32[512]{0:T(512)}, f32[512]{0:T(512)S(1)}, u32[]{:S(2)}) copy-start(f32[512]{0:T(512)S(1)} %get-tuple-element.135) | copy-start | bytes 6148

commit v2 on v1

--- a/solution.py
+++ b/solution.py
@@ -19,10 +19,9 @@
 SLOT = 64
 NS = NL * SLOT
 PAIRS = NL // 2
-NEAR_PAIRS = 6
-CAP_NEAR = 48
-CAP_FAR = 32
-BACK = 5
+NEAR_PAIRS = 7
+CAPS = ((32, 32), (48, 16))
+BACK = 6
 EXT = 640
 NEIGH = ((-1, 0), (1, 0), (0, -1), (0, 1), (-1, -1), (-1, 1), (1, -1), (1, 1))
 
@@ -46,7 +45,7 @@
     ys = np.full((EXT,), -1000.0, np.float32)
     ys[:count] = cells[:, 1]
     ycol = np.broadcast_to(ys[:, None], (EXT, 128))
-    yrow = np.broadcast_to(ys[None, :], (8, EXT))
+    yrow = ys[None, :]
     sel = np.zeros((384, CELLS), np.float32)
     at = 0
     for dx, dy in NEIGH:
@@ -80,6 +79,49 @@
     return lax.broadcasted_iota(jnp.int32, shape, dim).astype(F32)
 
 STEPS = 4
+
+
+def ring_pass(value, axis):
+    size = lax.axis_size(axis)
+    return lax.ppermute(value, axis, [(i, (i + 1) % size) for i in range(size)])
+
+
+def ring_gather(value):
+    size, me = lax.axis_size("lon"), lax.axis_index("lon")
+    rows = value.shape[0]
+
+    def step(k, carry):
+        block, out = carry
+        out = lax.dynamic_update_slice_in_dim(out, block, (me - k) % size * rows, 0)
+        return ring_pass(block, "lon"), out
+
+    out = jnp.zeros((size * rows,) + value.shape[1:], value.dtype)
+    return lax.fori_loop(0, size, step, (value, out))[1]
+
+
+def ring_scatter(value, rows):
+    size, me = lax.axis_size("lon"), lax.axis_index("lon")
+
+    def own(k):
+        return lax.dynamic_slice_in_dim(value, (me + size - 1 - k) % size * rows, rows, 0)
+
+    total = lax.fori_loop(1, size, lambda k, acc: ring_pass(acc, "lon") + own(k), own(0))
+    return total.astype(jnp.bfloat16)
+
+
+def ring_total(value):
+    for repeat in range(2):
+        for axis in ("lon", "lat"):
+            def step(k, carry):
+                block, total = carry
+                block = ring_pass(block, axis)
+                return block, total + block
+
+            value = lax.fori_loop(1, lax.axis_size(axis), step, (value, value))[1]
+        if repeat == 0:
+            first = jnp.logical_and(lax.axis_index("lon") == 0, lax.axis_index("lat") == 0)
+            value = jnp.where(first, value, 0.0)
+    return value
 
 
 def with_halo(value, sides, width, wrap):
@@ -140,7 +182,7 @@
     shifted, weights = corner_table(
         flat_ids.reshape(cells), frac_lon.reshape(cells), frac_lat.reshape(cells), lat_cells
     )
-    shard_piece = lax.all_gather(latent_state, "lon", axis=0, tiled=True)
+    shard_piece = ring_gather(latent_state)
     count = shard_piece.shape[0] * lat_cells
     local = shifted
     hits = local[:, :, None] == jnp.arange(count, dtype=jnp.int32)[None, None, :]
@@ -190,14 +232,9 @@
         jnp.bfloat16
     )
     term = jnp.einsum("ksr,ksc->rc", onehot, parts, preferred_element_type=jnp.float32)
-    summed = lax.psum_scatter(
-        term.reshape(count, lat_cells, chans).astype(jnp.bfloat16),
-        "lon",
-        scatter_dimension=0,
-        tiled=True,
-    )
-    grad_inner, grad_outer, grad_gain = lax.psum(
-        (local_inner, local_outer, local_gain), ("lon", "lat")
+    summed = ring_scatter(term.reshape(count, lat_cells, chans), lon_cells)
+    grad_inner, grad_outer, grad_gain = (
+        ring_total(v) for v in (local_inner, local_outer, local_gain)
     )
     return (state_out, summed, grad_inner, grad_outer, grad_gain)
 
@@ -205,10 +242,10 @@
 def kernel(
     lat_state, cot_ref, w_in, w_out, gain_ref, sb_ref, cc_ref, fa_ref, fb_ref, ter_ref, ktab,
     adj_ref, ycol_ref, yrow_ref, sel_ref, spread_ref,
-    out_ref, grad_ref, gout, vec_ref,
-    G, W_hi, W_lo, rows_out, rows_in, gro, gin, req_out, req_in, t_out, t_in,
-    ext_f, ext_b, stage_f, stage_b, gd_ref, Mh, Ml, M2h, M2l, Ah, Al, Bh, Bl,
-    z_ref, act_ref, gp_ref, gbuf, sib_in, hsum, rs_in, xh_out, xh_in, v_out, v_lat, v_sum, v_lon,
+    out_ref, grad_ref, gi_ref, go_ref, gg_ref, over_ref,
+    gout, G, W_hi, W_lo, rows_out, rows_in, gro, gin, req_out, req_in, t_out, t_in,
+    ext_f, ext_b, stage_f, stage_b, gd_ref, acc_ref, Mh, Ml, M2h, M2l, Ah, Al, Bh, Bl,
+    z_ref, p_ref, gp_ref, gbuf, sib_in, hsum, rs_in, xh_out, xh_in, v_out, v_lat, v_sum, v_lon,
     s_req, r_req, s_row, r_row, s_gro, r_gro, s_ter, r_ter, s_hf, r_hf, s_hb, r_hb,
     s_sib, r_sib, s_rs, r_rs, s_xh, r_xh, s_ag, r_ag, s_fin, r_fin, s_vl, r_vl, s_vn, r_vn,
 ):
@@ -217,6 +254,14 @@
     core = lax.rem(la, 2)
     sib = la + 1 - 2 * core
     opp = lax.rem(la + 2, NT)
+
+    inside = jnp.logical_and(la > 0, la < NT - 1)
+
+    def sized(far, body):
+        for kind, flag in ((0, jnp.logical_not(inside)), (1, inside)):
+            @pl.when(flag)
+            def _():
+                body(CAPS[kind][far])
 
     def lon_at(d):
         return lax.rem(me + d + 2 * NL, NL)
@@ -275,7 +320,9 @@
     before = (iota((CELLS, CELLS), 0) < iota((CELLS, CELLS), 1)).astype(F32).astype(BF16)
     counts = nn(jnp.where(hits, 1.0, 0.0).astype(BF16), before)
     rank = jnp.sum(jnp.where(hits, counts, 0.0), 0, keepdims=True)
-    cap = jnp.where(slot < 2.0 * NEAR_PAIRS, float(CAP_NEAR), float(CAP_FAR))
+    near_cap = jnp.where(inside, float(CAPS[1][0]), float(CAPS[0][0]))
+    far_cap = jnp.where(inside, float(CAPS[1][1]), float(CAPS[0][1]))
+    cap = jnp.where(slot < 2.0 * NEAR_PAIRS, near_cap, far_cap)
     fits = rank < cap
     place = jnp.where(fits, slot * float(SLOT) + rank, -1.0)
     over = jnp.sum(jnp.where(fits, 0.0, 1.0), axis=1, keepdims=True)
@@ -302,8 +349,12 @@
     params = rows_of(
         [cell, fah, fam, fa - fah - fam, fbh, fbm, fb - fbh - fbm, jnp.ones_like(fa)], 16, CELLS
     ).astype(BF16)
-    for p in range(PAIRS):
-        req_out[p] = nt(params, G[128 * p : 128 * p + 128, :])[0:8]
+
+    def fill_req(p, carry):
+        req_out[p] = nt(params, G[pl.ds(pl.multiple_of(p * 128, 128), 128), :])[0:8]
+        return carry
+
+    lax.fori_loop(0, PAIRS, fill_req, 0)
     t_all = nt(jnp.broadcast_to(ter, (16, CELLS)).astype(BF16), sel_ref[...])
     for q in range(3):
         t_out[q] = t_all[0:8, 128 * q : 128 * q + 128]
@@ -348,7 +399,7 @@
             s_row.at[j], r_row.at[j], lon_at(BACK - j), la,
         )
 
-    def make_rows(cap_j):
+    def make_rows(far):
         def body(p, carry):
             t = jnp.where(lane_low, req_in[2 * p], req_in[2 * p + 1])
             cid = t[0:1]
@@ -371,14 +422,14 @@
             for j in (2 * p, 2 * p + 1):
                 @pl.when(j != BACK)
                 def _():
-                    row_copy(j, cap_j).start()
+                    sized(far, lambda c: row_copy(j, c).start())
 
             return carry
 
         return body
 
-    lax.fori_loop(0, NEAR_PAIRS, make_rows(CAP_NEAR), 0)
-    lax.fori_loop(NEAR_PAIRS, PAIRS, make_rows(CAP_FAR), 0)
+    lax.fori_loop(0, NEAR_PAIRS, make_rows(0), 0)
+    lax.fori_loop(NEAR_PAIRS, PAIRS, make_rows(1), 0)
     own_rows = slice(BACK * SLOT, BACK * SLOT + SLOT)
     rows_in[own_rows, :] = rows_out[own_rows, :]
 
@@ -403,48 +454,67 @@
     kap = jnp.zeros((8, EXT), F32)
     for k in range(8):
         kap = kap + jnp.where(t_ext == float(k), ktab[k], 0.0)
-    kap = jnp.where((yr >= 0.0) & (yr < 64.0), kap, 0.0)[0:1]
-    for q in range(EXT // 128):
-        block = slice(128 * q, 128 * q + 128)
-        eye = iota((128, EXT), 0) + float(128 * q) == iota((128, EXT), 1)
+    kap = jnp.where((yr >= 0.0) & (yr < 64.0), kap[0:1], 0.0)
+    def blocks(count, body):
+        def step(q, carry):
+            body(pl.ds(pl.multiple_of(q * 128, 128), 128), q * 128)
+            return carry
+
+        lax.fori_loop(0, count, step, 0)
+
+    def fill_m(block, row):
+        eye = iota((128, EXT), 0) + lax.convert_element_type(row, F32) == iota((128, EXT), 1)
         m = adj_ref[block, :].astype(F32) * kap + jnp.where(eye, 1.0 - 4.0 * kap, 0.0)
         yc = ycol_ref[block, 0:1].astype(F32) + lat0
         m = jnp.where((yc >= 0.0) & (yc < 64.0), m, 0.0)
         Mh[block, :], Ml[block, :] = split2(m)
 
+    blocks(EXT // 128, fill_m)
+
     def prod(ah, al, bh, bl):
         return nn(ah, bh) + (nn(ah, bl) + nn(al, bh))
 
-    for q in range(EXT // 128):
-        block = slice(128 * q, 128 * q + 128)
+    def square(block, row):
         m2 = prod(Mh[block, :], Ml[block, :], Mh[...], Ml[...])
         M2h[block, :], M2l[block, :] = split2(m2)
-    for q in range(EXT // 128):
-        block = slice(128 * q, 128 * q + 128)
+
+    def last_a(block, row):
         v = prod(M2h[block, :], M2l[block, :], M2h[:, 0:CELLS], M2l[:, 0:CELLS])
         Ah[block, :], Al[block, :] = split2(v)
-    for q in range(CELLS // 128):
-        block = slice(128 * q, 128 * q + 128)
+
+    def last_b(block, row):
         v = prod(M2h[block, :], M2l[block, :], M2h[...], M2l[...])
         Bh[block, :], Bl[block, :] = split2(v)
+
+    blocks(EXT // 128, square)
+    blocks(EXT // 128, last_a)
+    blocks(CELLS // 128, last_b)
 
     def both_caps(body):
         def near(j, carry):
             @pl.when(j != BACK)
             def _():
-                body(j, CAP_NEAR)
+                sized(0, lambda c: body(j, c))
 
             return carry
 
         def far(j, carry):
-            body(j, CAP_FAR)
+            sized(1, lambda c: body(j, c))
             return carry
 
         lax.fori_loop(0, 2 * NEAR_PAIRS, near, 0)
         lax.fori_loop(2 * NEAR_PAIRS, NL, far, 0)
 
     both_caps(lambda j, c: row_copy(j, c).wait_recv())
-    ext_f[0:CELLS, :] = tn(G[...], rows_in[...]).astype(BF16)
+
+    def put_rows(k, acc):
+        part = pl.ds(pl.multiple_of(k * 512, 512), 512)
+        acc_ref[...] += tn(G[part, :], rows_in[part, :])
+        return acc
+
+    acc_ref[...] = jnp.zeros((CELLS, CH), F32)
+    lax.fori_loop(0, NS // 512, put_rows, 0)
+    ext_f[0:CELLS, :] = acc_ref[...].astype(BF16)
 
     def halo_copy(ext, stage, ssem, rsem, n):
         dx, dy = NEIGH[n]
@@ -472,26 +542,42 @@
         halo_copy(ext_f, stage_f, s_hf, r_hf, n).wait_recv()
     field = tn(Ah[...], ext_f[...]) + tn(Al[...], ext_f[...])
 
+    def sib_copy(k):
+        return send(gbuf.at[1 - core, k], sib_in.at[k], s_sib.at[k], r_sib.at[k], me, sib)
+
     gain = gain_ref[...]
     r = lax.rsqrt(jnp.mean(field * field, axis=1, keepdims=True) + 1e-06)
     normed = field * r
-    z = (normed * gain).astype(BF16)
-    z_ref[...] = z
+    z_ref[...] = (normed * gain).astype(BF16)
     cot = cot_ref[...]
-    react = jnp.zeros((CELLS, CH), F32)
-    gz = jnp.zeros((CELLS, CH), F32)
-    for h in range(4):
-        part = slice(256 * h, 256 * h + 256)
-        p = nn(z, w_in[:, part])
+    acc_ref[...] = field
+
+    def forward(h, carry):
+        part = pl.ds(pl.multiple_of(h * 256, 256), 256)
+        p = nn(z_ref[...], w_in[:, part])
+        p_ref[:, part] = p
+        act = (p * (1.0 / (1.0 + jnp.exp(-p)))).astype(BF16)
+        gbuf[h // 2, 1, pl.ds(lax.rem(h, 2) * 256, 256), :] = tn(act, cot_ref[...]).astype(BF16)
+        acc_ref[...] += nn(act, w_out[part, :])
+        return carry
+
+    lax.fori_loop(0, 4, forward, 0)
+    sib_copy(1).start()
+    out_ref[...] = acc_ref[...].astype(BF16)
+    acc_ref[...] = jnp.zeros((CELLS, CH), F32)
+
+    def backward(h, carry):
+        part = pl.ds(pl.multiple_of(h * 256, 256), 256)
+        ga = nt(cot_ref[...], w_out[part, :])
+        p = p_ref[:, part]
         sig = 1.0 / (1.0 + jnp.exp(-p))
-        act = (p * sig).astype(BF16)
-        act_ref[:, part] = act
-        react = react + nn(act, w_out[part, :])
-        ga = nt(cot, w_out[part, :])
         gp = (ga * sig * (1.0 + p * (1.0 - sig))).astype(BF16)
         gp_ref[:, part] = gp
-        gz = gz + nt(gp, w_in[:, part])
-    out_ref[...] = (field + react).astype(BF16)
+        acc_ref[...] += nt(gp, w_in[:, part])
+        return carry
+
+    lax.fori_loop(0, 4, backward, 0)
+    gz = acc_ref[...]
     ggain = jnp.sum(gz * normed, axis=0, keepdims=True)
     gn = gz * gain
     gfield = cot.astype(F32) + r * (gn - normed * jnp.mean(gn * normed, axis=1, keepdims=True))
@@ -499,12 +585,13 @@
     ext_b[0:CELLS, :] = g_hi
     halo_start(ext_b, stage_b, s_hb, r_hb)
 
-    for h in range(2):
-        half = slice(512 * h, 512 * h + 512)
+    def inner_half(h, carry):
+        half = pl.ds(pl.multiple_of(h * 512, 512), 512)
         gbuf[h, 0] = tn(z_ref[...], gp_ref[:, half]).astype(BF16)
-        gbuf[h, 1] = tn(act_ref[:, half], cot_ref[...]).astype(BF16)
-    sib_copy = send(gbuf.at[1 - core], sib_in, s_sib, r_sib, me, sib)
-    sib_copy.start()
+        return carry
+
+    lax.fori_loop(0, 2, inner_half, 0)
+    sib_copy(0).start()
     v_out[...] = rows_of(
         [ggain[:, 128 * k : 128 * k + 128] for k in range(4)] + [jnp.broadcast_to(over, (1, 128))],
         8, 128,
@@ -516,6 +603,27 @@
     for d in range(1, NT):
         vl_copy(d).start()
     v_lat[pl.ds(la, 1)] = v_out[...].reshape(1, 8, 128)
+
+    def rs_copy(d):
+        to = lon_at(d)
+        return send(
+            hsum.at[:, pl.ds(pl.multiple_of(to * 16, 16), 16), :], rs_in.at[d],
+            s_rs.at[d], r_rs.at[d], to, la,
+        )
+
+    def each_other(body):
+        def step(d, carry):
+            body(d)
+            return carry
+
+        lax.fori_loop(1, NL, step, 0)
+
+    for k in (1, 0):
+        sib_copy(k).wait_recv()
+        hsum[k] = (gbuf[core, k].astype(F32) + sib_in[k].astype(F32)).astype(BF16)
+    each_other(lambda d: rs_copy(d).start())
+    mine = pl.ds(pl.multiple_of(me * 16, 16), 16)
+    rs_in[0] = hsum[:, mine, :]
 
     for n in range(8):
         halo_copy(ext_b, stage_b, s_hb, r_hb, n).wait_recv()
@@ -530,45 +638,23 @@
             s_gro.at[j], r_gro.at[j], lon_at(j - BACK), la,
         )
 
-    def bucket(cap_j):
+    def bucket(far):
         def body(p, carry):
             row = pl.multiple_of(p * 128, 128)
             gro[pl.ds(row, 128), :] = nn(G[pl.ds(row, 128), :], gd_ref[...]).astype(BF16)
             for j in (2 * p, 2 * p + 1):
                 @pl.when(j != BACK)
                 def _():
-                    gro_copy(j, cap_j).start()
+                    sized(far, lambda c: gro_copy(j, c).start())
 
             return carry
 
         return body
 
     gd_ref[...] = gdrift
-    lax.fori_loop(0, NEAR_PAIRS, bucket(CAP_NEAR), 0)
-    lax.fori_loop(NEAR_PAIRS, PAIRS, bucket(CAP_FAR), 0)
+    lax.fori_loop(0, NEAR_PAIRS, bucket(0), 0)
+    lax.fori_loop(NEAR_PAIRS, PAIRS, bucket(1), 0)
     gin[own_rows, :] = gro[own_rows, :]
-
-    sib_copy.wait_recv()
-    for k in range(2):
-        hsum[k] = (gbuf[core, k].astype(F32) + sib_in[k].astype(F32)).astype(BF16)
-
-    def rs_copy(d):
-        to = lon_at(d)
-        return send(
-            hsum.at[:, pl.ds(pl.multiple_of(to * 16, 16), 16), :], rs_in.at[d],
-            s_rs.at[d], r_rs.at[d], to, la,
-        )
-
-    def each_other(body):
-        def step(d, carry):
-            body(d)
-            return carry
-
-        lax.fori_loop(1, NL, step, 0)
-
-    each_other(lambda d: rs_copy(d).start())
-    mine = pl.ds(pl.multiple_of(me * 16, 16), 16)
-    rs_in[0] = hsum[:, mine, :]
 
     for d in range(1, NT):
         vl_copy(d).wait_recv()
@@ -580,14 +666,10 @@
     each_other(lambda d: vn_copy(d).start())
     v_lon[pl.ds(me, 1)] = v_sum[...].reshape(1, 8, 128)
 
-    both_caps(lambda j, c: gro_copy(j, c).wait_recv())
-    grad_ref[...] = (nn(W_hi[...], gin[...]) + nn(W_lo[...], gin[...])).astype(BF16)
-
     each_other(lambda d: rs_copy(d).wait_recv())
-    acc = jnp.zeros((2, 16, CH), F32)
-    for d in range(NL):
-        acc = acc + rs_in[d].astype(F32)
-    xh_out[...] = acc
+    xh_out[...] = lax.fori_loop(
+        0, NL, lambda d, acc: acc + rs_in[d].astype(F32), jnp.zeros((2, 16, CH), F32)
+    )
     xh_copy = send(xh_out, xh_in, s_xh, r_xh, me, opp)
     xh_copy.start()
     xh_copy.wait_recv()
@@ -595,17 +677,54 @@
 
     def ag_copy(d):
         piece = gout.at[core, :, mine, :]
-        return send(piece, piece, s_ag.at[d], r_ag.at[d], lon_at(d), la)
+        return send(piece, piece, s_ag.at[d], r_ag.at[me], lon_at(d), la)
+
+    def ag_wait(q):
+        piece = gout.at[core, :, pl.ds(pl.multiple_of(q * 16, 16), 16), :]
+        send(piece, piece, s_ag.at[q], r_ag.at[q], q, la).wait_recv()
 
     each_other(lambda d: ag_copy(d).start())
+    both_caps(lambda j, c: gro_copy(j, c).wait_recv())
+
+    def scatter(k, carry):
+        part = pl.ds(pl.multiple_of(k * 512, 512), 512)
+        acc_ref[...] += nn(W_hi[:, part], gin[part, :]) + nn(W_lo[:, part], gin[part, :])
+        return carry
+
+    acc_ref[...] = jnp.zeros((CELLS, CH), F32)
+    lax.fori_loop(0, NS // 512, scatter, 0)
+    grad_ref[...] = acc_ref[...].astype(BF16)
+
     each_other(lambda d: vn_copy(d).wait_recv())
     total = v_lon[0]
     for k in range(1, NL):
         total = total + v_lon[k]
-    vec_ref[...] = total
-    each_other(lambda d: ag_copy(d).wait_recv())
-    fin = send(gout.at[core], gout.at[core], s_fin, r_fin, me, sib)
-    fin.start()
+    for k in range(4):
+        gg_ref[0:1, 128 * k : 128 * k + 128] = total[k : k + 1]
+    over_ref[...] = total[4:5, 0:1]
+
+    def fin_copy(c):
+        piece = gout.at[core, :, 128 * c : 128 * c + 128, :]
+        return send(piece, piece, s_fin.at[c], r_fin.at[c], me, sib)
+
+    def leave(half, c):
+        rows = slice(128 * c, 128 * c + 128)
+        left = pl.ds(pl.multiple_of(half * 512, 512), 512)
+        below = pl.ds(pl.multiple_of(half * 512 + 128 * c, 128), 128)
+        gi_ref[rows, left] = gout[half, 0, rows, :]
+        go_ref[below, :] = gout[half, 1, rows, :]
+
+    for c in range(4):
+        def arrive(q, carry):
+            @pl.when(q != me)
+            def _():
+                ag_wait(q)
+
+            return carry
+
+        lax.fori_loop(8 * c, 8 * c + 8, arrive, 0)
+        fin_copy(c).start()
+        leave(core, c)
 
     each_pair(lambda j: req_copy(j).wait_send())
     for n in range(8):
@@ -614,14 +733,19 @@
         halo_copy(ext_b, stage_b, s_hb, r_hb, n).wait_send()
     both_caps(lambda j, c: row_copy(j, c).wait_send())
     both_caps(lambda j, c: gro_copy(j, c).wait_send())
-    sib_copy.wait_send()
+    sib_copy(0).wait_send()
+    sib_copy(1).wait_send()
     for d in range(1, NT):
         vl_copy(d).wait_send()
     each_other(lambda d: rs_copy(d).wait_send())
     each_other(lambda d: vn_copy(d).wait_send())
     xh_copy.wait_send()
     each_other(lambda d: ag_copy(d).wait_send())
-    fin.wait()
+    for c in range(4):
+        piece = gout.at[1 - core, :, 128 * c : 128 * c + 128, :]
+        send(piece, piece, s_fin.at[c], r_fin.at[c], me, sib).wait_recv()
+        leave(1 - core, c)
+        fin_copy(c).wait_send()
 
 
 def step_kernel(state, cot, w_in, w_out, gain, sb, cc, fa, fb, ter, ktab):
@@ -630,17 +754,18 @@
     dma = lambda *s: pltpu.SemaphoreType.DMA(s)
     one = pltpu.SemaphoreType.DMA
     scratch = [
+        vm(2, 2, 512, 512),
         vm(NS, CELLS), vm(CELLS, NS), vm(CELLS, NS), vm(NS, CH), vm(NS, CH), vm(NS, CH), vm(NS, CH),
         vm(PAIRS, 8, 128, t=F32), vm(NL, 8, 128, t=F32), vm(3, 8, 128, t=F32), vm(8, 8, 128, t=F32),
-        vm(EXT, CH), vm(EXT, CH), vm(192, CH), vm(192, CH), vm(CELLS, CH),
+        vm(EXT, CH), vm(EXT, CH), vm(192, CH), vm(192, CH), vm(CELLS, CH), vm(CELLS, CH, t=F32),
         vm(EXT, EXT), vm(EXT, EXT), vm(EXT, EXT), vm(EXT, EXT),
         vm(EXT, CELLS), vm(EXT, CELLS), vm(CELLS, EXT), vm(CELLS, EXT),
-        vm(CELLS, CH), vm(CELLS, HID), vm(CELLS, HID),
+        vm(CELLS, CH), vm(CELLS, HID, t=F32), vm(CELLS, HID),
         vm(2, 2, 512, 512), vm(2, 512, 512), vm(2, 512, 512), vm(NL, 2, 16, 512),
         vm(2, 16, 512, t=F32), vm(2, 16, 512, t=F32),
         vm(8, 128, t=F32), vm(NT, 8, 128, t=F32), vm(8, 128, t=F32), vm(NL, 8, 128, t=F32),
         dma(NL), dma(NL), dma(NL), dma(NL), dma(NL), dma(NL), dma(8), dma(8), dma(8), dma(8),
-        dma(8), dma(8), one, one, dma(NL), dma(NL), one, one, dma(NL), dma(NL), one, one,
+        dma(8), dma(8), dma(2), dma(2), dma(NL), dma(NL), one, one, dma(NL), dma(NL), dma(4), dma(4),
         dma(NT), dma(NT), dma(NL), dma(NL),
     ]
     vmem = pl.BlockSpec(memory_space=pltpu.VMEM)
@@ -650,11 +775,13 @@
         out_shape=(
             jax.ShapeDtypeStruct((CELLS, CH), BF16),
             jax.ShapeDtypeStruct((CELLS, CH), BF16),
-            jax.ShapeDtypeStruct((2, 2, 512, 512), BF16),
-            jax.ShapeDtypeStruct((8, 128), F32),
+            jax.ShapeDtypeStruct((CH, HID), BF16),
+            jax.ShapeDtypeStruct((HID, CH), BF16),
+            jax.ShapeDtypeStruct((1, CH), F32),
+            jax.ShapeDtypeStruct((1, 1), F32),
         ),
         in_specs=[vmem] * 10 + [smem] + [vmem] * 5,
-        out_specs=(vmem,) * 4,
+        out_specs=(vmem,) * 6,
         scratch_shapes=scratch,
         compiler_params=pltpu.CompilerParams(
             collective_id=0, has_side_effects=True, vmem_limit_bytes=60 * 1024 * 1024
@@ -671,19 +798,20 @@
 
 def on_device(*args):
     state, cot = (v.reshape(CELLS, CH) for v in args[:2])
-    state_out, state_grad, grads, vec = step_kernel(state, cot, *args[2:])
-    over = vec[4, 0]
-
-    def fast(state_out, state_grad, grads, vec, *rest):
-        inner = grads[:, 0].transpose(1, 0, 2).reshape(CH, HID).astype(F32)
-        outer = grads[:, 1].reshape(HID, CH).astype(F32)
-        shape = (16, 16, CH)
-        return state_out.reshape(shape), state_grad.reshape(shape), inner, outer, vec[0:4].reshape(CH)
-
-    def general(state_out, state_grad, grads, vec, *rest):
-        return on_device_general(*rest)
-
-    return lax.cond(over > 0.0, general, fast, state_out, state_grad, grads, vec, *args)
+    state_out, state_grad, inner, outer, gain, over = step_kernel(state, cot, *args[2:])
+    over = over.reshape(())
+    shape = (16, 16, CH)
+
+    def general(*carry):
+        made = on_device_general(*args)
+        return (jnp.zeros_like(over), *(v.astype(BF16) for v in made[:4]), made[4])
+
+    carry = (
+        over, state_out.reshape(shape), state_grad.reshape(shape), inner, outer,
+        gain.reshape(CH),
+    )
+    carry = lax.while_loop(lambda c: c[0] > 0.0, lambda c: general(*c), carry)
+    return (carry[1], carry[2], carry[3].astype(F32), carry[4].astype(F32), carry[5])
 
 
 def solution(mesh):

time: 138 us -> 111 us (0.80)
  between operations: 14.8 us -> 0.74 us
  local copies, waits for them, and re-layouts: 12.9 us -> 2.03 us
  Pallas kernels: 107 us -> 101 us
  other arithmetic: 2.13 us -> 4.48 us
    unnamed x24 -> x21, local copies, waits for them, and re-layouts: 9.63 us -> 2.03 us
    pallas_call x1, Pallas kernels: 107 us -> 101 us  [step_kernel(): pl.pallas_call(kernel, out_shape=(jax.ShapeDtypeStruct((CELLS, CH), BF16)...]
    convert_element_type x1 -> x2, other arithmetic: 1.78 us -> 4.48 us  [the longest x1 2.88 us: on_device(): carry[3].astype(F32)]
    convert_element_type x1 -> x0, local copies, waits for them, and re-layouts: 1.49 us -> none  [fast(): inner = grads[:, 0].transpose(1, 0, 2).reshape(CH, HID).astype(F32)]
where the time goes in v2:
time: 111 us; the launch traced here: 109 us
  Pallas kernels  101 us (91%)
  other arithmetic  4.48 us (4%)
  local copies, waits for them, and re-layouts  2.03 us (2%)
    pallas_call x1, Pallas kernels, step_kernel(): pl.pallas_call(kernel, out_shape=(jax.ShapeDtypeStruct((CELLS, CH), BF16)...  101 us
    convert_element_type x1, other arithmetic, on_device(): carry[3].astype(F32)  2.88 us

profile of v2, /device:TPU:0, one launch (start us, length us, event | category | flops | bytes accessed | tf_op | source)
XLA Modules:
  0.0 108.8 jit_solution(12465686114640948623)
XLA Ops:
  0.6 0.0 copy-start.20
  0.6 0.0 copy-start.24
  0.7 0.0 copy-start.29
  0.7 0.0 copy-start.37
  0.7 0.0 copy-start.39
  0.7 100.7 %shard_map.191 = (bf16[256,512]{1,0:T(8,128)(2,1)}, bf16[256,512]{1,0:T(8,128)(2,1)}, bf16[512,1024]{1,0:T(8,128)(2,1)}, bf16[1024,512]{1,0:T(8,128)(2,1)}, f32[1,512]{1,0:T(1,128)}, /*index=5*/f32[1,1]{1,0:T(1,128)}) custom-call(bf16[256,512]{1,0:T(8,128)(2,1)} %bitcast.9.lat_state, bf16[256,512]{1,0:T(8,128)(2,1)} %bitcast.50, bf16[512,1024]{1,0:T(8,128)(2,1)} %w_in.1, ...), custom_call_target="tpu_custom_call" | custom-call | flops 12000000000 | bytes 8388608 | tf_op jit(solution)/shard_map/pallas_call | solution.py:773
  101.4 0.0 copy-done.20
  101.4 0.0 copy-done.24
  101.4 0.0 copy-done.29
  101.4 0.0 copy-done.37
  101.4 0.0 copy-done.39
  101.5 0.8 while.203
  102.3 0.0 copy-start.28
  102.3 2.9 %convert_element_type.136 = f32[512,1024]{1,0:T(8,128)} convert(bf16[512,1024]{1,0:T(8,128)(2,1)} %get-tuple-element.1581) | non-fusion elementwise | flops 524288 | bytes 3145728 | tf_op jit(solution)/shard_map/convert_element_type | solution.py:814
  105.2 0.0 copy-start.35
  105.2 0.0 copy-start.36
  105.2 0.0 copy-done.28
  105.2 0.0 copy-start.27
  105.2 1.6 %convert_element_type.137 = f32[1024,512]{1,0:T(8,128)} convert(bf16[1024,512]{1,0:T(8,128)(2,1)S(1)} %copy-done.28) | non-fusion elementwise | flops 524288 | bytes 3145728 | tf_op jit(solution)/shard_map/convert_element_type | solution.py:814
  106.8 0.0 copy-done.35
  106.8 0.7 copy.169
  107.5 0.0 copy-done.36
  107.5 0.7 copy.170
  108.2 0.0 copy-done.27
  108.2 0.6 copy.171
Async XLA Ops:
  0.6 100.8 %copy-start.20 = (bf16[512,1024]{1,0:T(8,128)(2,1)S(1)}, bf16[512,1024]{1,0:T(8,128)(2,1)}, u32[]{:S(2)}) copy-start(bf16[512,1024]{1,0:T(8,128)(2,1)} %w_in.1) | copy-start | bytes 3145732
  0.6 100.8 %copy-start.24 = (bf16[16,16,512]{2,1,0:T(8,128)(2,1)S(1)}, bf16[16,16,512]{2,1,0:T(8,128)(2,1)}, u32[]{:S(2)}) copy-start(bf16[16,16,512]{2,1,0:T(8,128)(2,1)} %param.47) | copy-start | bytes 786436
  0.7 100.8 %copy-start.29 = (f32[512]{0:T(512)S(1)}, f32[512]{0:T(512)}, u32[]{:S(2)}) copy-start(f32[512]{0:T(512)} %param.50) | copy-start | bytes 6148
  0.7 100.8 %copy-start.37 = (s32[16,16]{1,0:T(8,128)S(1)}, s32[16,16]{1,0:T(8,128)}, u32[]{:S(2)}) copy-start(s32[16,16]{1,0:T(8,128)} %ter_ref.1) | copy-start | bytes 3076
  0.7 100.8 %copy-start.39 = (f32[8]{0:T(128)S(1)}, f32[8]{0:T(128)}, u32[]{:S(2)}) copy-start(f32[8]{0:T(128)} %ktab.1) | copy-start | bytes 100
  102.3 2.9 %copy-start.28 = (bf16[1024,512]{1,0:T(8,128)(2,1)S(1)}, bf16[1024,512]{1,0:T(8,128)(2,1)}, u32[]{:S(2)}) copy-start(bf16[1024,512]{1,0:T(8,128)(2,1)} %get-tuple-element.1582) | copy-start | bytes 3145732
  105.2 1.6 %copy-start.35 = (bf16[16,16,512]{2,1,0:T(8,128)(2,1)S(1)}, bf16[16,16,512]{2,1,0:T(8,128)(2,1)}, u32[]{:S(2)}) copy-start(bf16[16,16,512]{2,1,0:T(8,128)(2,1)} %get-tuple-element.1579) | copy-start | bytes 786436
  105.2 2.3 %copy-start.36 = (bf16[16,16,512]{2,1,0:T(8,128)(2,1)S(1)}, bf16[16,16,512]{2,1,0:T(8,128)(2,1)}, u32[]{:S(2)}) copy-start(bf16[16,16,512]{2,1,0:T(8,128)(2,1)} %get-tuple-element.1580) | copy-start | bytes 786436
  105.2 3.0 %copy-start.27 = (f32[512]{0:T(512)S(1)}, f32[512]{0:T(512)}, u32[]{:S(2)}) copy-start(f32[512]{0:T(512)} %get-tuple-element.1583) | copy-start | bytes 6148

commit v3 on v2

--- a/solution.py
+++ b/solution.py
@@ -244,8 +244,8 @@
     adj_ref, ycol_ref, yrow_ref, sel_ref, spread_ref,
     out_ref, grad_ref, gi_ref, go_ref, gg_ref, over_ref,
     gout, G, W_hi, W_lo, rows_out, rows_in, gro, gin, req_out, req_in, t_out, t_in,
-    ext_f, ext_b, stage_f, stage_b, gd_ref, acc_ref, Mh, Ml, M2h, M2l, Ah, Al, Bh, Bl,
-    z_ref, p_ref, gp_ref, gbuf, sib_in, hsum, rs_in, xh_out, xh_in, v_out, v_lat, v_sum, v_lon,
+    ext_f, ext_b, stage_f, stage_b, gd_ref, Mh, Ml, M2h, M2l, Ah, Al, Bh, Bl,
+    z_ref, slope_ref, gp_ref, gbuf, sib_in, hsum, rs_in, xh_out, xh_in, v_out, v_lat, v_sum, v_lon,
     s_req, r_req, s_row, r_row, s_gro, r_gro, s_ter, r_ter, s_hf, r_hf, s_hb, r_hb,
     s_sib, r_sib, s_rs, r_rs, s_xh, r_xh, s_ag, r_ag, s_fin, r_fin, s_vl, r_vl, s_vn, r_vn,
 ):
@@ -262,6 +262,12 @@
             @pl.when(flag)
             def _():
                 body(CAPS[kind][far])
+
+    def slot_sized(j, body):
+        for far, flag in ((0, j < 2 * NEAR_PAIRS), (1, j >= 2 * NEAR_PAIRS)):
+            @pl.when(jnp.logical_and(flag, j != BACK))
+            def _():
+                sized(far, body)
 
     def lon_at(d):
         return lax.rem(me + d + 2 * NL, NL)
@@ -399,37 +405,39 @@
             s_row.at[j], r_row.at[j], lon_at(BACK - j), la,
         )
 
-    def make_rows(far):
-        def body(p, carry):
-            t = jnp.where(lane_low, req_in[2 * p], req_in[2 * p + 1])
-            cid = t[0:1]
-            a = t[1:2] + t[2:3] + t[3:4]
-            b = t[4:5] + t[5:6] + t[6:7]
-            real = t[7:8]
-            at = iota((CELLS, 128), 0) - cid
-            w = (
-                jnp.where(at == 0.0, (1.0 - a) * (1.0 - b) * real, 0.0)
-                + jnp.where(at == 16.0, a * (1.0 - b) * real, 0.0)
-                + jnp.where(at == 1.0, (1.0 - a) * b * real, 0.0)
-                + jnp.where(at == 17.0, a * b * real, 0.0)
-            )
-            hi, lo = split2(w)
-            col = pl.multiple_of(p * 128, 128)
-            W_hi[:, pl.ds(col, 128)] = hi
-            W_lo[:, pl.ds(col, 128)] = lo
-            v = lat_state[...]
-            rows_out[pl.ds(col, 128), :] = (tn(hi, v) + tn(lo, v)).astype(BF16)
-            for j in (2 * p, 2 * p + 1):
-                @pl.when(j != BACK)
-                def _():
-                    sized(far, lambda c: row_copy(j, c).start())
-
+    def weigh(p):
+        t = jnp.where(lane_low, req_in[2 * p], req_in[2 * p + 1])
+        cid = t[0:1]
+        a = t[1:2] + t[2:3] + t[3:4]
+        b = t[4:5] + t[5:6] + t[6:7]
+        real = t[7:8]
+        at = iota((CELLS, 128), 0) - cid
+        w = (
+            jnp.where(at == 0.0, (1.0 - a) * (1.0 - b) * real, 0.0)
+            + jnp.where(at == 16.0, a * (1.0 - b) * real, 0.0)
+            + jnp.where(at == 1.0, (1.0 - a) * b * real, 0.0)
+            + jnp.where(at == 17.0, a * b * real, 0.0)
+        )
+        col = pl.ds(pl.multiple_of(p * 128, 128), 128)
+        W_hi[:, col], W_lo[:, col] = split2(w)
+
+    def start_group(g, copy):
+        def step(j, carry):
+            slot_sized(j, lambda c: copy(j, c).start())
             return carry
 
-        return body
-
-    lax.fori_loop(0, NEAR_PAIRS, make_rows(0), 0)
-    lax.fori_loop(NEAR_PAIRS, PAIRS, make_rows(1), 0)
+        lax.fori_loop(8 * g, 8 * g + 8, step, 0)
+
+    def make_rows(g, carry):
+        for k in range(4):
+            weigh(4 * g + k)
+        part = pl.ds(pl.multiple_of(g * 512, 512), 512)
+        v = lat_state[...]
+        rows_out[part, :] = (tn(W_hi[:, part], v) + tn(W_lo[:, part], v)).astype(BF16)
+        start_group(g, row_copy)
+        return carry
+
+    lax.fori_loop(0, 4, make_rows, 0)
     own_rows = slice(BACK * SLOT, BACK * SLOT + SLOT)
     rows_in[own_rows, :] = rows_out[own_rows, :]
 
@@ -506,15 +514,7 @@
         lax.fori_loop(2 * NEAR_PAIRS, NL, far, 0)
 
     both_caps(lambda j, c: row_copy(j, c).wait_recv())
-
-    def put_rows(k, acc):
-        part = pl.ds(pl.multiple_of(k * 512, 512), 512)
-        acc_ref[...] += tn(G[part, :], rows_in[part, :])
-        return acc
-
-    acc_ref[...] = jnp.zeros((CELLS, CH), F32)
-    lax.fori_loop(0, NS // 512, put_rows, 0)
-    ext_f[0:CELLS, :] = acc_ref[...].astype(BF16)
+    ext_f[0:CELLS, :] = tn(G[...], rows_in[...]).astype(BF16)
 
     def halo_copy(ext, stage, ssem, rsem, n):
         dx, dy = NEIGH[n]
@@ -549,35 +549,26 @@
     r = lax.rsqrt(jnp.mean(field * field, axis=1, keepdims=True) + 1e-06)
     normed = field * r
     z_ref[...] = (normed * gain).astype(BF16)
+    z = z_ref[...]
     cot = cot_ref[...]
-    acc_ref[...] = field
-
-    def forward(h, carry):
-        part = pl.ds(pl.multiple_of(h * 256, 256), 256)
-        p = nn(z_ref[...], w_in[:, part])
-        p_ref[:, part] = p
-        act = (p * (1.0 / (1.0 + jnp.exp(-p)))).astype(BF16)
-        gbuf[h // 2, 1, pl.ds(lax.rem(h, 2) * 256, 256), :] = tn(act, cot_ref[...]).astype(BF16)
-        acc_ref[...] += nn(act, w_out[part, :])
-        return carry
-
-    lax.fori_loop(0, 4, forward, 0)
+    react = jnp.zeros((CELLS, CH), F32)
+    for h in range(4):
+        part = slice(256 * h, 256 * h + 256)
+        p = nn(z, w_in[:, part])
+        sig = 1.0 / (1.0 + jnp.exp(-p))
+        act = (p * sig).astype(BF16)
+        slope_ref[:, part] = sig * (1.0 + p * (1.0 - sig))
+        half = slice(256 * (h % 2), 256 * (h % 2) + 256)
+        gbuf[h // 2, 1, half, :] = tn(act, cot).astype(BF16)
+        react = react + nn(act, w_out[part, :])
     sib_copy(1).start()
-    out_ref[...] = acc_ref[...].astype(BF16)
-    acc_ref[...] = jnp.zeros((CELLS, CH), F32)
-
-    def backward(h, carry):
-        part = pl.ds(pl.multiple_of(h * 256, 256), 256)
-        ga = nt(cot_ref[...], w_out[part, :])
-        p = p_ref[:, part]
-        sig = 1.0 / (1.0 + jnp.exp(-p))
-        gp = (ga * sig * (1.0 + p * (1.0 - sig))).astype(BF16)
+    out_ref[...] = (field + react).astype(BF16)
+    gz = jnp.zeros((CELLS, CH), F32)
+    for h in range(4):
+        part = slice(256 * h, 256 * h + 256)
+        gp = (nt(cot, w_out[part, :]) * slope_ref[:, part]).astype(BF16)
         gp_ref[:, part] = gp
-        acc_ref[...] += nt(gp, w_in[:, part])
-        return carry
-
-    lax.fori_loop(0, 4, backward, 0)
-    gz = acc_ref[...]
+        gz = gz + nt(gp, w_in[:, part])
     ggain = jnp.sum(gz * normed, axis=0, keepdims=True)
     gn = gz * gain
     gfield = cot.astype(F32) + r * (gn - normed * jnp.mean(gn * normed, axis=1, keepdims=True))
@@ -638,22 +629,14 @@
             s_gro.at[j], r_gro.at[j], lon_at(j - BACK), la,
         )
 
-    def bucket(far):
-        def body(p, carry):
-            row = pl.multiple_of(p * 128, 128)
-            gro[pl.ds(row, 128), :] = nn(G[pl.ds(row, 128), :], gd_ref[...]).astype(BF16)
-            for j in (2 * p, 2 * p + 1):
-                @pl.when(j != BACK)
-                def _():
-                    sized(far, lambda c: gro_copy(j, c).start())
-
-            return carry
-
-        return body
+    def bucket(g, carry):
+        part = pl.ds(pl.multiple_of(g * 512, 512), 512)
+        gro[part, :] = nn(G[part, :], gd_ref[...]).astype(BF16)
+        start_group(g, gro_copy)
+        return carry
 
     gd_ref[...] = gdrift
-    lax.fori_loop(0, NEAR_PAIRS, bucket(0), 0)
-    lax.fori_loop(NEAR_PAIRS, PAIRS, bucket(1), 0)
+    lax.fori_loop(0, 4, bucket, 0)
     gin[own_rows, :] = gro[own_rows, :]
 
     for d in range(1, NT):
@@ -685,16 +668,7 @@
 
     each_other(lambda d: ag_copy(d).start())
     both_caps(lambda j, c: gro_copy(j, c).wait_recv())
-
-    def scatter(k, carry):
-        part = pl.ds(pl.multiple_of(k * 512, 512), 512)
-        acc_ref[...] += nn(W_hi[:, part], gin[part, :]) + nn(W_lo[:, part], gin[part, :])
-        return carry
-
-    acc_ref[...] = jnp.zeros((CELLS, CH), F32)
-    lax.fori_loop(0, NS // 512, scatter, 0)
-    grad_ref[...] = acc_ref[...].astype(BF16)
-
+    grad_ref[...] = (nn(W_hi[...], gin[...]) + nn(W_lo[...], gin[...])).astype(BF16)
     each_other(lambda d: vn_copy(d).wait_recv())
     total = v_lon[0]
     for k in range(1, NL):
@@ -757,7 +731,7 @@
         vm(2, 2, 512, 512),
         vm(NS, CELLS), vm(CELLS, NS), vm(CELLS, NS), vm(NS, CH), vm(NS, CH), vm(NS, CH), vm(NS, CH),
         vm(PAIRS, 8, 128, t=F32), vm(NL, 8, 128, t=F32), vm(3, 8, 128, t=F32), vm(8, 8, 128, t=F32),
-        vm(EXT, CH), vm(EXT, CH), vm(192, CH), vm(192, CH), vm(CELLS, CH), vm(CELLS, CH, t=F32),
+        vm(EXT, CH), vm(EXT, CH), vm(192, CH), vm(192, CH), vm(CELLS, CH),
         vm(EXT, EXT), vm(EXT, EXT), vm(EXT, EXT), vm(EXT, EXT),
         vm(EXT, CELLS), vm(EXT, CELLS), vm(CELLS, EXT), vm(CELLS, EXT),
         vm(CELLS, CH), vm(CELLS, HID, t=F32), vm(CELLS, HID),

time: 111 us -> 109 us (0.982)
  Pallas kernels: 101 us -> 98.3 us
    pallas_call x1, Pallas kernels: 101 us -> 98.3 us  [step_kernel(): pl.pallas_call(kernel, out_shape=(jax.ShapeDtypeStruct((CELLS, CH), BF16)...]
where the time goes in v3:
time: 109 us; the launch traced here: 106 us
  Pallas kernels  98.3 us (90%)
  other arithmetic  4.48 us (4%)
  local copies, waits for them, and re-layouts  2.03 us (2%)
    pallas_call x1, Pallas kernels, step_kernel(): pl.pallas_call(kernel, out_shape=(jax.ShapeDtypeStruct((CELLS, CH), BF16)...  98.3 us
    convert_element_type x1, other arithmetic, on_device(): carry[3].astype(F32)  2.88 us

profile of v3, /device:TPU:0, one launch (start us, length us, event | category | flops | bytes accessed | tf_op | source)
XLA Modules:
  0.0 106.4 jit_solution(14184617140936426304)
XLA Ops:
  0.6 0.0 copy-start.20
  0.6 0.0 copy-start.24
  0.7 0.0 copy-start.29
  0.7 0.0 copy-start.37
  0.7 0.0 copy-start.39
  0.7 98.3 %shard_map.191 = (bf16[256,512]{1,0:T(8,128)(2,1)}, bf16[256,512]{1,0:T(8,128)(2,1)}, bf16[512,1024]{1,0:T(8,128)(2,1)}, bf16[1024,512]{1,0:T(8,128)(2,1)}, f32[1,512]{1,0:T(1,128)}, /*index=5*/f32[1,1]{1,0:T(1,128)}) custom-call(bf16[256,512]{1,0:T(8,128)(2,1)} %bitcast.9.lat_state, bf16[256,512]{1,0:T(8,128)(2,1)} %bitcast.50, bf16[512,1024]{1,0:T(8,128)(2,1)} %w_in.1, ...), custom_call_target="tpu_custom_call" | custom-call | flops 12000000000 | bytes 8388608 | tf_op jit(solution)/shard_map/pallas_call | solution.py:747
  99.0 0.0 copy-done.20
  99.0 0.0 copy-done.24
  99.1 0.0 copy-done.29
  99.1 0.0 copy-done.37
  99.1 0.0 copy-done.39
  99.1 0.8 while.203
  99.9 0.0 copy-start.28
  99.9 2.9 %convert_element_type.136 = f32[512,1024]{1,0:T(8,128)} convert(bf16[512,1024]{1,0:T(8,128)(2,1)} %get-tuple-element.1581) | non-fusion elementwise | flops 524288 | bytes 3145728 | tf_op jit(solution)/shard_map/convert_element_type | solution.py:788
  102.8 0.0 copy-start.35
  102.8 0.0 copy-start.36
  102.8 0.0 copy-done.28
  102.8 0.0 copy-start.27
  102.8 1.6 %convert_element_type.137 = f32[1024,512]{1,0:T(8,128)} convert(bf16[1024,512]{1,0:T(8,128)(2,1)S(1)} %copy-done.28) | non-fusion elementwise | flops 524288 | bytes 3145728 | tf_op jit(solution)/shard_map/convert_element_type | solution.py:788
  104.4 0.0 copy-done.35
  104.4 0.7 copy.169
  105.1 0.0 copy-done.36
  105.1 0.7 copy.170
  105.8 0.0 copy-done.27
  105.8 0.6 copy.171
Async XLA Ops:
  0.6 98.4 %copy-start.20 = (bf16[512,1024]{1,0:T(8,128)(2,1)S(1)}, bf16[512,1024]{1,0:T(8,128)(2,1)}, u32[]{:S(2)}) copy-start(bf16[512,1024]{1,0:T(8,128)(2,1)} %w_in.1) | copy-start | bytes 3145732
  0.6 98.4 %copy-start.24 = (bf16[16,16,512]{2,1,0:T(8,128)(2,1)S(1)}, bf16[16,16,512]{2,1,0:T(8,128)(2,1)}, u32[]{:S(2)}) copy-start(bf16[16,16,512]{2,1,0:T(8,128)(2,1)} %param.47) | copy-start | bytes 786436
  0.7 98.4 %copy-start.29 = (f32[512]{0:T(512)S(1)}, f32[512]{0:T(512)}, u32[]{:S(2)}) copy-start(f32[512]{0:T(512)} %param.50) | copy-start | bytes 6148
  0.7 98.4 %copy-start.37 = (s32[16,16]{1,0:T(8,128)S(1)}, s32[16,16]{1,0:T(8,128)}, u32[]{:S(2)}) copy-start(s32[16,16]{1,0:T(8,128)} %ter_ref.1) | copy-start | bytes 3076
  0.7 98.4 %copy-start.39 = (f32[8]{0:T(128)S(1)}, f32[8]{0:T(128)}, u32[]{:S(2)}) copy-start(f32[8]{0:T(128)} %ktab.1) | copy-start | bytes 100
  99.9 2.9 %copy-start.28 = (bf16[1024,512]{1,0:T(8,128)(2,1)S(1)}, bf16[1024,512]{1,0:T(8,128)(2,1)}, u32[]{:S(2)}) copy-start(bf16[1024,512]{1,0:T(8,128)(2,1)} %get-tuple-element.1582) | copy-start | bytes 3145732
  102.8 1.6 %copy-start.35 = (bf16[16,16,512]{2,1,0:T(8,128)(2,1)S(1)}, bf16[16,16,512]{2,1,0:T(8,128)(2,1)}, u32[]{:S(2)}) copy-start(bf16[16,16,512]{2,1,0:T(8,128)(2,1)} %get-tuple-element.1579) | copy-start | bytes 786436
  102.8 2.3 %copy-start.36 = (bf16[16,16,512]{2,1,0:T(8,128)(2,1)S(1)}, bf16[16,16,512]{2,1,0:T(8,128)(2,1)}, u32[]{:S(2)}) copy-start(bf16[16,16,512]{2,1,0:T(8,128)(2,1)} %get-tuple-element.1580) | copy-start | bytes 786436
  102.8 3.0 %copy-start.27 = (f32[512]{0:T(512)S(1)}, f32[512]{0:T(512)}, u32[]{:S(2)}) copy-start(f32[512]{0:T(512)} %get-tuple-element.1583) | copy-start | bytes 6148

commit v4 on v3

--- a/solution.py
+++ b/solution.py
@@ -531,10 +531,8 @@
         )
 
     def halo_start(ext, stage, ssem, rsem):
-        for n in range(2):
-            halo_copy(ext, stage, ssem, rsem, n).start()
         stage[...] = nn(sel_ref[128:320, :], ext[0:CELLS, :]).astype(BF16)
-        for n in range(2, 8):
+        for n in (2, 3, 4, 5, 6, 7, 0, 1):
             halo_copy(ext, stage, ssem, rsem, n).start()
 
     halo_start(ext_f, stage_f, s_hf, r_hf)

time: 109 us -> 107 us (0.982); the launches traced: 106 us -> 106 us
  no operation moved by 1% of the time
where the time goes in v4:
time: 107 us; the launch traced here: 106 us
  Pallas kernels  97.6 us (91%)
  other arithmetic  4.48 us (4%)
  local copies, waits for them, and re-layouts  2.03 us (2%)
    pallas_call x1, Pallas kernels, step_kernel(): pl.pallas_call(kernel, out_shape=(jax.ShapeDtypeStruct((CELLS, CH), BF16)...  97.6 us
    convert_element_type x1, other arithmetic, on_device(): carry[3].astype(F32)  2.88 us

profile of v4, /device:TPU:0, one launch (start us, length us, event | category | flops | bytes accessed | tf_op | source)
XLA Modules:
  0.0 105.7 jit_solution(1954085399813415220)
XLA Ops:
  0.6 0.0 copy-start.20
  0.6 0.0 copy-start.24
  0.7 0.0 copy-start.29
  0.7 0.0 copy-start.37
  0.7 0.0 copy-start.39
  0.7 97.6 %shard_map.191 = (bf16[256,512]{1,0:T(8,128)(2,1)}, bf16[256,512]{1,0:T(8,128)(2,1)}, bf16[512,1024]{1,0:T(8,128)(2,1)}, bf16[1024,512]{1,0:T(8,128)(2,1)}, f32[1,512]{1,0:T(1,128)}, /*index=5*/f32[1,1]{1,0:T(1,128)}) custom-call(bf16[256,512]{1,0:T(8,128)(2,1)} %bitcast.9.lat_state, bf16[256,512]{1,0:T(8,128)(2,1)} %bitcast.50, bf16[512,1024]{1,0:T(8,128)(2,1)} %w_in.1, ...), custom_call_target="tpu_custom_call" | custom-call | flops 12000000000 | bytes 8388608 | tf_op jit(solution)/shard_map/pallas_call | solution.py:745
  98.3 0.0 copy-done.20
  98.4 0.0 copy-done.24
  98.4 0.0 copy-done.29
  98.4 0.0 copy-done.37
  98.4 0.0 copy-done.39
  98.4 0.8 while.203
  99.2 0.0 copy-start.28
  99.2 2.9 %convert_element_type.136 = f32[512,1024]{1,0:T(8,128)} convert(bf16[512,1024]{1,0:T(8,128)(2,1)} %get-tuple-element.1581) | non-fusion elementwise | flops 524288 | bytes 3145728 | tf_op jit(solution)/shard_map/convert_element_type | solution.py:786
  102.1 0.0 copy-start.35
  102.1 0.0 copy-start.36
  102.1 0.0 copy-done.28
  102.1 0.0 copy-start.27
  102.1 1.6 %convert_element_type.137 = f32[1024,512]{1,0:T(8,128)} convert(bf16[1024,512]{1,0:T(8,128)(2,1)S(1)} %copy-done.28) | non-fusion elementwise | flops 524288 | bytes 3145728 | tf_op jit(solution)/shard_map/convert_element_type | solution.py:786
  103.7 0.0 copy-done.35
  103.7 0.7 copy.169
  104.4 0.0 copy-done.36
  104.4 0.7 copy.170
  105.1 0.0 copy-done.27
  105.2 0.6 copy.171
Async XLA Ops:
  0.6 97.7 %copy-start.20 = (bf16[512,1024]{1,0:T(8,128)(2,1)S(1)}, bf16[512,1024]{1,0:T(8,128)(2,1)}, u32[]{:S(2)}) copy-start(bf16[512,1024]{1,0:T(8,128)(2,1)} %w_in.1) | copy-start | bytes 3145732
  0.6 97.7 %copy-start.24 = (bf16[16,16,512]{2,1,0:T(8,128)(2,1)S(1)}, bf16[16,16,512]{2,1,0:T(8,128)(2,1)}, u32[]{:S(2)}) copy-start(bf16[16,16,512]{2,1,0:T(8,128)(2,1)} %param.47) | copy-start | bytes 786436
  0.7 97.7 %copy-start.29 = (f32[512]{0:T(512)S(1)}, f32[512]{0:T(512)}, u32[]{:S(2)}) copy-start(f32[512]{0:T(512)} %param.50) | copy-start | bytes 6148
  0.7 97.7 %copy-start.37 = (s32[16,16]{1,0:T(8,128)S(1)}, s32[16,16]{1,0:T(8,128)}, u32[]{:S(2)}) copy-start(s32[16,16]{1,0:T(8,128)} %ter_ref.1) | copy-start | bytes 3076
  0.7 97.7 %copy-start.39 = (f32[8]{0:T(128)S(1)}, f32[8]{0:T(128)}, u32[]{:S(2)}) copy-start(f32[8]{0:T(128)} %ktab.1) | copy-start | bytes 100
  99.2 2.9 %copy-start.28 = (bf16[1024,512]{1,0:T(8,128)(2,1)S(1)}, bf16[1024,512]{1,0:T(8,128)(2,1)}, u32[]{:S(2)}) copy-start(bf16[1024,512]{1,0:T(8,128)(2,1)} %get-tuple-element.1582) | copy-start | bytes 3145732
  102.1 1.6 %copy-start.35 = (bf16[16,16,512]{2,1,0:T(8,128)(2,1)S(1)}, bf16[16,16,512]{2,1,0:T(8,128)(2,1)}, u32[]{:S(2)}) copy-start(bf16[16,16,512]{2,1,0:T(8,128)(2,1)} %get-tuple-element.1579) | copy-start | bytes 786436
  102.1 2.3 %copy-start.36 = (bf16[16,16,512]{2,1,0:T(8,128)(2,1)S(1)}, bf16[16,16,512]{2,1,0:T(8,128)(2,1)}, u32[]{:S(2)}) copy-start(bf16[16,16,512]{2,1,0:T(8,128)(2,1)} %get-tuple-element.1580) | copy-start | bytes 786436
  102.1 3.0 %copy-start.27 = (f32[512]{0:T(512)S(1)}, f32[512]{0:T(512)}, u32[]{:S(2)}) copy-start(f32[512]{0:T(512)} %get-tuple-element.1583) | copy-start | bytes 6148
